TPU v7x, 256 devices: a whole 4x4x8 slice. The times are simulated.
256 devices in a mesh: grp: 8 (over x, core), seg: 32 (over z, y).
Axes of the slice: x: 4, y: 4, z: 8, core: 2. Of those that a mesh axis runs over, the one named last changes fastest.
Arguments:
- frames: bfloat16 [2048, 64, 192], P(('grp', 'seg')), may hold values from -6 to 6
- conv_first: bfloat16 [4, 4, 3, 64], replicated, may hold values from -0.875 to 0.875
- second_kernel_weight: bfloat16 [4, 4, 64, 128], replicated, may hold values from -0.25 to 0.25
- conv_third: bfloat16 [4, 4, 128, 256], replicated, may hold values from -0.1875 to 0.1875
- observe_map: bfloat16 [256, 256], replicated, may hold values from -0.375 to 0.375
- skew_source: float32 [256, 256], replicated, may hold values from -0.375 to 0.375
- retain: float32 [2048, 256], P(('grp', 'seg')), may hold values from 0 to 1
Outputs:
- filtered: float32 [2048, 256], P(('grp', 'seg'))
All inputs are finite; a program needn't handle non-finite values.
Results may differ from a plain program's by a relative error of at most 0.004.
Values sent between devices are 32-bit elements; how exact they have to be, the bound alone decides.
No kernel may reach another device: no remote copies, remote signals or barrier semaphores. Data moves between devices by JAX's collectives and lax.ppermute only.
A program may use at most 192 MiB of HBM per device.

v0:
```python
import jax
import jax.numpy as jnp
from jax import lax
from jax.sharding import PartitionSpec as P

TAYLOR = 8


def entering(value, axis, join, neutral):
    count, mine = (lax.axis_size(axis), lax.axis_index(axis))
    pieces = jax.tree.map(lambda part: lax.all_gather(part, axis), value)
    running = jax.tree.map(
        lambda part, zero: jnp.full_like(part, 0) + jnp.asarray(zero, part.dtype), value, neutral
    )

    def turn(position, running):
        longer = join(running, jax.tree.map(lambda part: part[position], pieces))
        return jax.tree.map(lambda new, old: jnp.where(position < mine, new, old), longer, running)

    return lax.fori_loop(0, count - 1, turn, running)


def make_rotation(skew_source, total_frames):
    skew = (skew_source - skew_source.T) * (0.7 / jnp.sqrt(jnp.float32(total_frames)))
    eye_matrix = jnp.eye(skew.shape[0], dtype=jnp.float32)
    term = eye_matrix
    total = eye_matrix
    for order in range(1, TAYLOR + 1):
        term = jnp.dot(term, skew, precision=lax.Precision.HIGHEST) / order
        total = total + term
    return total


def apply_convolution(inputs, kernel):
    return lax.conv_general_dilated(
        inputs,
        kernel,
        (2, 2),
        ((1, 1), (1, 1)),
        dimension_numbers=("NHWC", "HWIO", "NHWC"),
        preferred_element_type=jnp.float32,
    )


def encode(frames, conv_first, second_kernel_weight, conv_third):
    count = frames.shape[0]
    pixels = frames.reshape(count, frames.shape[1], frames.shape[1], 3)
    first = jax.nn.relu(apply_convolution(pixels, conv_first)).astype(jnp.bfloat16)
    second = jax.nn.relu(apply_convolution(first, second_kernel_weight)).astype(jnp.bfloat16)
    third = jax.nn.relu(apply_convolution(second, conv_third))
    return jnp.mean(third, axis=(1, 2)).astype(jnp.bfloat16)


def compose(earlier, later):
    early_map, early_shift = earlier
    late_map, late_shift = later
    joined_map = jnp.dot(late_map, early_map, precision=lax.Precision.HIGHEST)
    joined_shift = jnp.dot(late_map, early_shift, precision=lax.Precision.HIGHEST) + late_shift
    return (joined_map, joined_shift)


def on_device(
    frames, conv_first, second_kernel_weight, conv_third, observe_map, skew_source, retain
):
    local_frames = frames.shape[0]
    width = retain.shape[1]
    device_count = lax.axis_size("grp") * lax.axis_size("seg")
    total_frames = local_frames * device_count
    rotation = make_rotation(skew_source, total_frames)
    pooled = encode(frames, conv_first, second_kernel_weight, conv_third)
    drive = (1.0 - retain) * jnp.dot(pooled, observe_map, preferred_element_type=jnp.float32)

    def advance(carry, inputs):
        prefix_map, prefix_shift = carry
        keep, push = inputs
        prefix_map = keep[:, None] * jnp.dot(rotation, prefix_map, precision=lax.Precision.HIGHEST)
        prefix_shift = (
            keep * jnp.dot(rotation, prefix_shift, precision=lax.Precision.HIGHEST) + push
        )
        return ((prefix_map, prefix_shift), (prefix_map, prefix_shift))

    eye_matrix = jnp.eye(width, dtype=jnp.float32)
    zero_state = jnp.zeros((width,), jnp.float32)
    own, stacked = lax.scan(advance, (eye_matrix, zero_state), (retain, drive))
    identity_matrix = (eye_matrix, zero_state)
    entry_map, entry_state = entering(own, ("grp", "seg"), compose, identity_matrix)
    prefix_maps, prefix_shifts = stacked
    passed_along = jnp.einsum(
        "tij,j->ti", prefix_maps, entry_state, precision=lax.Precision.HIGHEST
    )
    filtered = prefix_shifts + passed_along
    return filtered


def solution(mesh):
    placed = (P(("grp", "seg"), None, None), P(), P(), P(), P(), P(), P(("grp", "seg"), None))
    return jax.shard_map(
        on_device, mesh=mesh, in_specs=placed, out_specs=P(("grp", "seg"), None), check_vma=False
    )
```

profile of v0, /device:TPU:6, one launch (start us, length us, event | category | flops | bytes accessed | tf_op | source)
XLA Modules:
  0.0 609.1 jit_solution(13386193917212700389)
XLA Ops:
  12.1 4.6 copy.17
  16.7 10.0 %fusion.7 = bf16[8,16,16,128]{3,0,2,1:T(8,128)(2,1)S(1)} fusion(bf16[4,4,64,128]{3,2,1,0:T(8,128)(2,1)S(1)} %copy-done.5, bf16[8,64,64,3]{0,3,2,1:T(4,128)(2,1)} %copy.17, bf16[4,4,3,64]{3,1,2,0:T(4,128)(2,1)S(1)} %copy-done.6), kind=kOutput, calls=%fused_computation.17 | convolution fusion | flops 554184704 | bytes 989184 | tf_op jit(solution)/shard_map/conv_general_dilated | solution.py:35
  27.7 12.0 %while.31 = (s32[]{:T(128)}, f32[256,256]{1,0:T(8,128)S(1)}, f32[256]{0:T(256)S(1)}, f32[8,256,256]{2,1,0:T(8,128)}, f32[8,256]{1,0:T(8,128)S(1)}, /*index=5*/f3...) while((s32[]{:T(128)}, f32[256,256]{1,0:T(8,128)S(1)}, ...), condition=%wide.region_2.3_spmd.clone, body=%wide.region_1.2_spmd.clone.sunk | while | flops 202179328 | bytes 1850999 | solution.py:84
  40.4 66.2 %all-gather.2 = f32[256,1,256]{2,1,0:T(1,128)S(1)} all-gather(f32[1,1,256]{2,1,0:T(1,128)S(1)} %bitcast.88), channel_id=3, replica_groups=mesh['grp'=8,'seg'=32] {'grp','seg'}, dimensions={0}, use_global_device_ids=true | all-gather | bytes 263168 | tf_op jit(solution)/shard_map/all_gather | solution.py:11
  106.6 149.3 %all-gather.5.cloned.1.call-done = f32[65536,256]{1,0:T(8,128)} async-done(((f32[256,256]{1,0:T(8,128)}), f32[65536,256]{1,0:T(8,128)}) %all-gather.5.cloned.1.call-update) | async-done | bytes 67108880 | tf_op jit(solution)/shard_map/all_gather | solution.py:11
  255.9 342.2 %while.32 = (s32[]{:T(128)}, f32[256]{0:T(256)S(1)}, s32[]{:T(128)}, f32[256,256,256]{2,1,0:T(8,128)}, f32[256,256]{1,0:T(8,128)S(1)}, /*index=5*/s32[]{:T(128)}, s32[]{:T(128)}) while((s32[]{:T(128)}, f32[256]{0:T(256)S(1)}, s32[]{:T(128)}, f32[256,256,256]{2,1,0:T(8,128)}, f32[256,256]{1,0:T(8,128)S(1)}, /*index=5*/s32[]{:T(128)}, ...), condition=%wide.region_4.5_spmd.clone, body=%wide.region_3.4_spmd.clone.sunk | while | flops 787460 | bytes 272998 | solution.py:20
  257.3 1.2 fusion.62
  258.6 1.2 fusion.62
  262.7 1.2 fusion.62
  264.0 1.2 fusion.62
  268.0 1.2 fusion.62
  269.4 1.2 fusion.62
  273.4 1.2 fusion.62
  274.7 1.2 fusion.62
  278.8 1.2 fusion.62
  280.1 1.2 fusion.62
  282.8 1.2 fusion.62
  284.1 1.2 fusion.62
  288.2 1.2 fusion.62
  289.5 1.2 fusion.62
  293.5 1.2 fusion.62
  294.9 1.2 fusion.62
  298.9 1.2 fusion.62
  300.2 1.2 fusion.62
  304.3 1.2 fusion.62
  305.6 1.2 fusion.62
  308.3 1.2 fusion.62
  309.6 1.2 fusion.62
  313.7 1.2 fusion.62
  315.0 1.2 fusion.62
  319.0 1.2 fusion.62
  598.2 3.4 fusion.19
  (1087 shorter events, 321.1 us)
Async XLA Ops:
  6.5 20.1 %copy-start = (bf16[4,4,128,256]{3,2,1,0:T(8,128)(2,1)S(1)}, bf16[4,4,128,256]{3,2,1,0:T(8,128)(2,1)}, u32[]{:S(2)}) copy-start(bf16[4,4,128,256]{3,2,1,0:T(8,128)(2,1)} %param.14) | copy-start | bytes 3145732
  6.5 249.4 %all-gather.5.cloned.1.call-start = ((), (), s32[]{:S(2)}) async-start(), calls=%async_computation | async-start | bytes 67371008 | tf_op jit(solution)/shard_map/all_gather | solution.py:11
  10.6 1.2 copy-start.2
  12.0 4.6 copy-start.5
  12.1 4.6 copy-start.6
  26.6 0.9 copy-start.3
  26.7 0.9 copy-start.4
  39.7 0.7 copy-start.1
Sparse Core Ops, SparseCore 0:
  40.5 215.3 all-gather.4
where the time goes:
time: 619 us; the launch traced here: 609 us
  matrix products  340 us (55%)
  waiting for transfers between devices  149 us (24%)
  blocking collectives  66.2 us (11%)
  local copies, waits for them, and re-layouts  23.2 us (4%)
  between operations  13.6 us (2%)
  loops' own time  10.3 us (2%)
    dot_general x255, matrix products, compose(): jnp.dot(late_map, early_shift, precision=lax.Precision.HIGHEST) + late_shift  312 us
    all_gather x1, waiting for transfers between devices, entering(): pieces = jax.tree.map(lambda part: lax.all_gather(part, axis), value)  149 us
    all_gather x1, blocking collectives, entering(): pieces = jax.tree.map(lambda part: lax.all_gather(part, axis), value)  66.2 us
    dynamic_slice x255, local copies, waits for them, and re-layouts, turn(): longer = join(running, jax.tree.map(lambda part: part[position], pieces))  15.4 us
  transfers between devices with their start and end apart: 1, of which 1 were waited for; matrix products, arithmetic and copies ran while one was open for 0% of the time, Pallas kernels for 0%

commit v1 on v0

v1 whole, which is shorter than its diff:
```python
import functools

import jax
import jax.numpy as jnp
import numpy as np
from jax import lax
from jax.experimental import pallas as pl
from jax.experimental.pallas import tpu as pltpu
from jax.sharding import Mesh, PartitionSpec as P

VMEM = pl.BlockSpec(memory_space=pltpu.VMEM)
LIMIT = 40 * 1024 * 1024
F32, BF16 = jnp.float32, jnp.bfloat16


def halves(value):
    top = value.astype(BF16)
    return top, (value - top.astype(F32)).astype(BF16)


def dot3(left, right):
    (left_top, left_rest), (right_top, right_rest) = left, right
    return (
        jnp.dot(left_top, right_rest, preferred_element_type=F32)
        + jnp.dot(left_rest, right_top, preferred_element_type=F32)
    ) + jnp.dot(left_top, right_top, preferred_element_type=F32)


def product(left, right):
    return dot3(halves(left), halves(right))


def call(kernel, outs, scratch, flops, traffic, *args):
    return pl.pallas_call(
        kernel,
        out_shape=[jax.ShapeDtypeStruct(shape, kind) for shape, kind in outs],
        in_specs=[VMEM] * len(args),
        out_specs=[VMEM] * len(outs),
        scratch_shapes=[pltpu.VMEM(shape, kind) for shape, kind in scratch],
        compiler_params=pltpu.CompilerParams(vmem_limit_bytes=LIMIT),
        cost_estimate=pl.CostEstimate(flops=flops, bytes_accessed=traffic, transcendentals=0),
    )(*args)


def rows_of(store, step, first, length):
    ways = store.shape[0]
    pieces = []
    for turn in range(ways // step):
        row = first + step * turn
        pieces.append(store[row % ways, pl.ds(row // ways, length * step // ways)])
    return pieces


def put_rows(store, value, first, start, size):
    ways = store.shape[0]
    share = value.shape[0] // ways
    for turn in range(ways):
        row = first + turn
        store[row % ways, pl.ds(row // ways, share), :, start : start + size] = value[turn * share : (turn + 1) * share]


def clear_rows(store, rows):
    for row in rows:
        store[row % store.shape[0], row // store.shape[0]] = jnp.zeros(store.shape[2:], F32)


def flatten(pieces, start, size):
    return jnp.concatenate([p[:, :, start : start + size].reshape(-1, size) for p in pieces], 0).astype(BF16)


def encoder_kernel(frames, band, second, third, observe, retain, drive, flat, lines, wide, one, two):
    count, height, row = frames.shape
    lanes = lines.shape[3]
    pixels = frames[...].astype(F32).reshape(count * height, row)
    pixels = jnp.concatenate([pixels, jnp.zeros((count * height, lanes - row), F32)], 1)
    pixels = pltpu.roll(pixels, 9, 1)
    flat[0] = pixels[:, :128]
    flat[1] = pixels[:, 128:]
    clear_rows(lines, (0, height + 1))
    for h in range(height):
        for side in range(2):
            picked = flat[side, pl.ds(h, count, stride=height), :]
            lines[(h + 1) % 8, (h + 1) // 8, :, 128 * side : 128 * side + 128] = picked
    taps, depth, broad = band.shape
    room = lanes - depth
    wide[...] = jnp.zeros_like(wide)
    for tap in range(taps):
        wide[tap, room : room + depth, :] = band[tap]

    rows = height // 2
    clear_rows(one, (0, rows + 1))
    sources = [flatten(rows_of(lines, 2, tap, rows), 0, lanes) for tap in range(taps)]
    total = one.shape[3]
    for start in range(0, total, broad):
        size = min(broad, total - start)
        shift = start // broad * 48
        value = jnp.zeros((rows * count, size), F32)
        for tap in range(taps):
            weights = wide[tap, room - shift : room - shift + lanes, :size]
            value += jnp.dot(sources[tap], weights, preferred_element_type=F32)
        value = jnp.maximum(value, 0.0).astype(BF16).astype(F32)
        lane = lax.broadcasted_iota(jnp.int32, value.shape, 1) + start
        if start == 0:
            value = jnp.where(lane >= 64, value, 0.0)
        if start + size == total:
            value = jnp.where(lane < total - 64, value, 0.0)
        put_rows(one, value.reshape(rows, count, size), 1, start, size)

    rows = rows // 2
    clear_rows(two, (0, rows + 1))
    edge = jnp.zeros(two.shape[:3] + (128,), F32)
    two[:, :, :, :128] = edge
    two[:, :, :, two.shape[3] - 128 :] = edge
    group = 4
    for left in range(0, rows, group):
        value = jnp.zeros((group * rows * count, 128), F32)
        for tap in range(4):
            pieces = []
            for j in range(left, left + group):
                pieces.append(flatten([p[:, :, 128 * j : 128 * j + 256] for p in rows_of(one, 2, tap, rows)], 0, 256))
            value += jnp.dot(jnp.concatenate(pieces, 0), second[tap], preferred_element_type=F32)
        value = jnp.maximum(value, 0.0).astype(BF16).astype(F32).reshape(group, rows, count, 128)
        for k in range(group):
            put_rows(two, value[k], 1, 128 * (left + k + 1), 128)

    rows = rows // 2
    value = jnp.zeros((rows * rows * count, third.shape[2]), F32)
    for tap in range(4):
        pieces = [flatten(rows_of(two, 2, tap, rows), 256 * j, 512) for j in range(rows)]
        value += jnp.dot(jnp.concatenate(pieces, 0), third[tap], preferred_element_type=F32)
    value = jnp.maximum(value, 0.0).reshape(rows * rows, count, value.shape[1])
    pooled = (jnp.sum(value, 0) * (1.0 / (rows * rows))).astype(BF16)
    drive[...] = (1.0 - retain[...]) * jnp.dot(pooled, observe[...], preferred_element_type=F32)


def encode(frames, conv_first, second_kernel_weight, conv_third, observe_map, retain):
    count, height, row = frames.shape
    taps = conv_first.reshape(4, 12, 64)
    band = jnp.stack([jnp.pad(taps, ((0, 0), (6 * k, 52 - 6 * k), (0, 0))) for k in range(8)], 2).reshape(4, 64, 512)
    (drive,) = call(
        encoder_kernel,
        [(retain.shape, F32)],
        [
            ((2, count * height, 128), F32),
            ((8, height // 8 + 1, count, 256), F32),
            ((4, 448, 512), BF16),
            ((4, height // 8 + 1, count, 34 * 64), F32),
            ((2, height // 8 + 1, count, 18 * 128), F32),
        ],
        4 * 10**9,
        4 * 10**6,
        frames,
        band,
        second_kernel_weight.reshape(4, 256, 128),
        conv_third.reshape(4, 512, 256),
        observe_map,
        retain,
    )
    return drive


def order(pieces, place):
    count = len(pieces)
    me = lax.axis_index("y")
    for shift, piece in enumerate(pieces):
        slot = lax.rem(me - shift + count, count)
        place[pl.ds(slot, 1)] = piece[...][None]


def turn_kernel(factor, source, top, rest):
    width = source.shape[0]
    skew = (source[...].T - source[...]) * factor
    first = halves(skew)
    two = dot3(first, first)
    square = halves(two)
    three = dot3(first, square)
    four = dot3(square, square)
    row = lax.broadcasted_iota(jnp.int32, (width, width), 0)
    eye = (row == lax.broadcasted_iota(jnp.int32, (width, width), 1)).astype(F32)
    upper = eye / 24.0 + skew / 120.0 + two / 720.0 + three / 5040.0 + four / 40320.0
    turn = skew + two / 2.0 + three / 6.0 + product(four, upper)
    top[...], rest[...] = halves(turn)


def maps_kernel(top, rest, *refs):
    pieces, (maps, block, own, keeps) = refs[:-4], refs[-4:]
    count = len(pieces)
    order(pieces, keeps)
    local, width = pieces[0].shape
    turn = (top[...], rest[...])
    row = lax.broadcasted_iota(jnp.int32, (width, width), 0)
    eye = (row == lax.broadcasted_iota(jnp.int32, (width, width), 1)).astype(F32)
    start = eye + (turn[0].astype(F32) + turn[1].astype(F32))
    values = [start * keeps[b, 0:1, :] for b in range(count)]
    for step in range(1, local):
        values = [(v + dot3(halves(v), turn)) * keeps[b, step : step + 1, :] for b, v in enumerate(values)]
    for b in range(count):
        maps[b] = values[b]
    me = lax.axis_index("y")
    before, mine = values[0], eye
    for b in range(1, count):
        mine = jnp.where(me == b, before, mine)
        before = product(before, values[b])
    own[...] = mine
    block[...] = before


def local_kernel(top, rest, maps, *refs):
    count = maps.shape[0]
    keep_pieces, push_pieces = refs[:count], refs[count : 2 * count]
    end, entry, keeps, pushes = refs[2 * count :]
    order(keep_pieces, keeps)
    order(push_pieces, pushes)
    turn = (top[...], rest[...])
    state = jnp.concatenate([pushes[b, 0:1, :] for b in range(count)] * 2, 0)
    for step in range(1, keeps.shape[1]):
        keep = jnp.concatenate([keeps[b, step : step + 1, :] for b in range(count)] * 2, 0)
        push = jnp.concatenate([pushes[b, step : step + 1, :] for b in range(count)] * 2, 0)
        state = (state + dot3(halves(state), turn)) * keep + push
    me = lax.axis_index("y")
    width = state.shape[1]
    spread = lambda b: jnp.broadcast_to(state[b : b + 1], (8, width))
    before, mine = spread(0), jnp.zeros((8, width), F32)
    for b in range(1, count):
        mine = jnp.where(me == b, before, mine)
        before = product(before, maps[b]) + spread(b)
    end[...] = before
    entry[...] = mine


def final_kernel(top, rest, entry, own_map, own_entry, retain, drive, out):
    turn = (top[...], rest[...])
    state = product(entry[...], own_map[...]) + own_entry[...]
    rows = []
    for step in range(retain.shape[0]):
        state = (state + dot3(halves(state), turn)) * retain[step : step + 1, :] + drive[step : step + 1, :]
        rows.append(state[0:1])
    out[...] = jnp.concatenate(rows, 0)


def dot(a, b):
    return jnp.dot(a, b, precision=lax.Precision.HIGH, preferred_element_type=F32)


def around(value, axis, count):
    return [value] + [lax.ppermute(value, axis, [(i, (i + k) % count) for i in range(count)]) for k in range(1, count)]


def exchange_pairs(bit, count):
    if 2 * bit == count:
        return [(i, count - 1 - i) for i in range(count)]
    return [(i, i ^ bit) for i in range(count)]


def on_device(frames, conv_first, second_kernel_weight, conv_third, observe_map, skew_source, retain):
    local, width = retain.shape
    count_x, count_y, count_z = lax.axis_size("x"), lax.axis_size("y"), lax.axis_size("z")
    total_frames = local * count_x * count_y * count_z * lax.axis_size("core")
    me_x = lax.axis_index("x")
    square, vector = (width, width), (8, width)

    keeps = around(retain, "y", count_y)
    factor = float(np.float32(0.7) / np.sqrt(np.float32(total_frames)))
    top, rest = call(functools.partial(turn_kernel, factor), [(square, BF16)] * 2, [], 10**9, 10**6, skew_source)
    drive = encode(frames, conv_first, second_kernel_weight, conv_third, observe_map, retain)
    pushes = around(drive, "y", count_y)

    top, rest, _ = lax.optimization_barrier((top, rest, drive))
    maps, block_map, own_map = call(
        maps_kernel,
        [((count_y,) + square, F32), (square, F32), (square, F32)],
        [((count_y, local, width), F32)],
        4 * 10**9,
        2 * 10**6,
        top,
        rest,
        *keeps,
    )
    block_end, own_entry = call(
        local_kernel,
        [(vector, F32)] * 2,
        [((count_y, local, width), F32)] * 2,
        10**9,
        2 * 10**6,
        top,
        rest,
        maps,
        *keeps,
        *pushes,
    )

    levels = [("z", 1 << k, count_z) for k in range(count_z.bit_length() - 1)] + [("core", 1, 2)]
    for axis, bit, count in levels:
        pairs = exchange_pairs(bit, count)
        upper = (lax.axis_index(axis) & bit) > 0
        other_end = lax.ppermute(block_end[:1], axis, pairs)
        other_map = lax.ppermute(block_map, axis, pairs)
        low = jnp.where(upper, other_map, block_map)
        high = jnp.where(upper, block_map, other_map)
        low_end = jnp.where(upper, other_end, block_end[:1])
        high_end = jnp.where(upper, block_end[:1], other_end)
        own_entry = jnp.where(upper, dot(low_end, own_map) + own_entry, own_entry)
        own_map = jnp.where(upper, dot(low, own_map), own_map)
        block_end = dot(low_end, high) + high_end
        block_map = dot(low, high)

    entry = jnp.zeros((1, width), F32)
    leaving = block_end
    for hop in range(count_x - 1):
        arrived = lax.ppermute(leaving, "x", [(hop, hop + 1)])
        entry = jnp.where(me_x == hop + 1, arrived, entry)
        if hop + 2 < count_x:
            leaving = dot(entry, block_map) + block_end

    (filtered,) = call(
        final_kernel,
        [((local, width), F32)],
        [],
        10**8,
        10**6,
        top,
        rest,
        jnp.broadcast_to(entry, vector),
        own_map,
        own_entry,
        retain,
        drive,
    )
    return filtered


def solution(mesh):
    grp, seg = mesh.shape["grp"], mesh.shape["seg"]
    parts = Mesh(mesh.devices.reshape(grp // 2, 2, seg // 4, 4), ("x", "core", "z", "y"))
    whole = ("x", "core", "z", "y")
    placed = (P(whole), P(), P(), P(), P(), P(), P(whole))
    return jax.shard_map(on_device, mesh=parts, in_specs=placed, out_specs=P(whole), check_vma=False)
```

time: 619 us -> 79.6 us (0.13); the launches traced: 609 us -> 79.4 us
  matrix products: 340 us -> 3.73 us
  waiting for transfers between devices: 149 us -> 37.5 us
  blocking collectives: 66.2 us -> 0 us
  starting transfers between devices: 0.01 us -> 22.4 us
  local copies, waits for them, and re-layouts: 23.2 us -> 2.43 us
  between operations: 13.6 us -> 0.29 us
  Pallas kernels: 0 us -> 13.1 us
  loops' own time: 10.3 us -> 0 us
    dot_general x281 -> x18, matrix products: 330 us -> 3.73 us  [dot(): jnp.dot(a, b, precision=lax.Precision.HIGH, preferred_element_type=F32)]
    all_gather x1 -> x0, waiting for transfers between devices: 149 us -> none  [entering(): pieces = jax.tree.map(lambda part: lax.all_gather(part, axis), value)]
    all_gather x1 -> x0, blocking collectives: 66.2 us -> none  [entering(): pieces = jax.tree.map(lambda part: lax.all_gather(part, axis), value)]
    ppermute x0 -> x17, waiting for transfers between devices: none -> 37.5 us  [the longest x4 23.8 us: on_device(): other_map = lax.ppermute(block_map, axis, pairs)]
    ppermute x0 -> x17, starting transfers between devices: none -> 22.4 us  [the longest x6 8.84 us: around(): lax.ppermute(value, axis, [(i, (i + k) % count) for i in range(count)])]
    dynamic_slice x263 -> x0, local copies, waits for them, and re-layouts: 15.5 us -> none  [the longest x255 15.4 us: turn(): longer = join(running, jax.tree.map(lambda part: part[position], pieces))]
    pallas_call x0 -> x5, Pallas kernels: none -> 13.1 us  [call(): pl.pallas_call(kernel, out_shape=[jax.ShapeDtypeStruct(shape, kind) for s...]
    conv_general_dilated x2 -> x0, matrix products: 10.7 us -> none  [apply_convolution(): lax.conv_general_dilated(inputs, kernel, (2, 2), ((1, 1), (1, 1)), dimens...]
  transfers between devices with their start and end apart: 1 -> 17, of which waited for: 1 -> 7; matrix products, arithmetic and copies ran while one was open for 0% -> 6% of each run, Pallas kernels for 0% -> 14%
where the time goes in v1:
time: 79.6 us; the launch traced here: 79.4 us
  waiting for transfers between devices  37.5 us (47%)
  starting transfers between devices  22.4 us (28%)
  Pallas kernels  13.1 us (16%)
  matrix products  3.73 us (5%)
  local copies, waits for them, and re-layouts  2.43 us (3%)
    ppermute x4, waiting for transfers between devices, on_device(): other_map = lax.ppermute(block_map, axis, pairs)  23.8 us
    pallas_call x5, Pallas kernels, call(): pl.pallas_call(kernel, out_shape=[jax.ShapeDtypeStruct(shape, kind) for s...  13.1 us
    ppermute x3, waiting for transfers between devices, on_device(): arrived = lax.ppermute(leaving, 'x', [(hop, hop + 1)])  9.21 us
    ppermute x6, starting transfers between devices, around(): lax.ppermute(value, axis, [(i, (i + k) % count) for i in range(count)])  8.84 us
    ppermute x4, starting transfers between devices, on_device(): other_end = lax.ppermute(block_end[:1], axis, pairs)  8 us
    ppermute x4, waiting for transfers between devices, on_device(): other_end = lax.ppermute(block_end[:1], axis, pairs)  4.48 us
    dot_general x18, matrix products, dot(): jnp.dot(a, b, precision=lax.Precision.HIGH, preferred_element_type=F32)  3.73 us
    ppermute x4, starting transfers between devices, on_device(): other_map = lax.ppermute(block_map, axis, pairs)  2.79 us
  transfers between devices with their start and end apart: 17, of which 7 were waited for; matrix products, arithmetic and copies ran while one was open for 6% of the time, Pallas kernels for 14%

profile of v1, /device:TPU:6, one launch (start us, length us, event | category | flops | bytes accessed | tf_op | source)
XLA Modules:
  0.0 79.4 jit_solution(5308297819950900632)
XLA Ops:
  0.0 3.0 %collective-permute-start.2 = (f32[8,256]{1,0:T(8,128)}, f32[8,256]{1,0:T(8,128)S(1)}, u32[]{:S(2)}, u32[]{:S(2)}) collective-permute-start(f32[8,256]{1,0:T(8,128)} %retain.3), channel_id=1, source_target_pairs={{0,3},{1,0},{2,1},{3,2},{4,7},{5,4},{6,5},{7,6},{8,11},{9,8},{10,9... | collective-permute-start | bytes 24584 | tf_op jit(solution)/shard_map/ppermute | solution.py:246
  3.0 0.6 collective-permute-start.1
  3.6 1.0 %collective-permute-start = (f32[8,256]{1,0:T(8,128)}, f32[8,256]{1,0:T(8,128)S(1)}, u32[]{:S(2)}, u32[]{:S(2)}) collective-permute-start(f32[8,256]{1,0:T(8,128)} %retain.3), channel_id=1, source_target_pairs={{0,1},{1,2},{2,3},{3,0},{4,5},{5,6},{6,7},{7,4},{8,9},{9,10},{10,1... | collective-permute-start | bytes 24584 | tf_op jit(solution)/shard_map/ppermute | solution.py:246
  4.6 0.7 copy.15
  5.6 0.3 copy.18
  6.0 0.3 reshape.49.band
  6.3 0.4 copy-done.1
  7.1 4.5 %shard_map.74.refs_4_.drive = f32[8,256]{1,0:T(8,128)S(1)} custom-call(bf16[8,64,192]{2,1,0:T(8,128)(2,1)S(1)} %copy-done.2, bf16[4,64,512]{2,1,0:T(8,128)(2,1)S(1)} %reshape.49.band, bf16[4,256,128]{2,1,0:T(8,128)(2,1)S(1)} %bitcast.75, bf16[4,512,256]{2,1,0:T(8,128)(2,1)S(1)} %bitcast.74, bf16[256,256]{1,0:T(8,128)(2,1)S(1)} %copy-done.5, f32[8,256]{1,0:T(8,128)S(1)} %copy-done), custom_call_target="tpu_custom_call" | custom-call | flops 4000000000 | bytes 4000000 | tf_op jit(solution)/shard_map/pallas_call | solution.py:34
  11.6 2.3 %collective-permute-start.5 = (f32[8,256]{1,0:T(8,128)S(1)}, f32[8,256]{1,0:T(8,128)S(1)}, u32[]{:S(2)}, u32[]{:S(2)}) collective-permute-start(f32[8,256]{1,0:T(8,128)S(1)} %shard_map.74.refs_4_.drive), channel_id=1, source_target_pairs={{0,3},{1,0},{2,1},{3,2},{4,7},{5,4},{6,5},{7,6},{8,11},{9,8},{10,9... | collective-permute-start | bytes 24584 | tf_op jit(solution)/shard_map/ppermute | solution.py:246
  13.8 1.7 %collective-permute-start.4 = (f32[8,256]{1,0:T(8,128)S(1)}, f32[8,256]{1,0:T(8,128)S(1)}, u32[]{:S(2)}, u32[]{:S(2)}) collective-permute-start(f32[8,256]{1,0:T(8,128)S(1)} %shard_map.74.refs_4_.drive), channel_id=1, source_target_pairs={{0,2},{1,3},{2,0},{3,1},{4,6},{5,7},{6,4},{7,5},{8,10},{9,11},{10,... | collective-permute-start | bytes 24584 | tf_op jit(solution)/shard_map/ppermute | solution.py:246
  15.5 1.1 %shard_map.73 = (bf16[256,256]{1,0:T(8,128)(2,1)S(1)}, bf16[256,256]{1,0:T(8,128)(2,1)S(1)}) custom-call(f32[256,256]{1,0:T(8,128)S(1)} %copy-done.4), custom_call_target="tpu_custom_call" | custom-call | flops 1000000000 | bytes 1000000 | tf_op jit(solution)/shard_map/pallas_call | solution.py:34
  17.0 3.9 %shard_map.75 = (f32[4,256,256]{2,1,0:T(8,128)S(1)}, f32[256,256]{1,0:T(8,128)S(1)}, f32[256,256]{1,0:T(8,128)S(1)}) custom-call(bf16[256,256]{1,0:T(8,128)(2,1)S(1)} %get-tuple-element.16.top, bf16[256,256]{1,0:T(8,128)(2,1)S(1)} %get-tuple-element.17.rest, f32[8,256]{1,0:T(8,128)S(1)} %copy-done, f32[8,256]{1,0:T(8,128)S(1)} %collective-permute-done.refs_1_, ...), custom_call_target="tpu_custom_call" | custom-call | flops 4000000000 | bytes 2000000 | tf_op jit(solution)/shard_map/pallas_call | solution.py:34
  20.9 2.0 %collective-permute-start.7 = (f32[256,256]{1,0:T(8,128)S(1)}, f32[256,256]{1,0:T(8,128)S(1)}, u32[]{:S(2)}, u32[]{:S(2)}) collective-permute-start(f32[256,256]{1,0:T(8,128)S(1)} %get-tuple-element.20), channel_id=1, source_target_pairs={{0,4},{4,0},{8,12},{12,8},{16,20},{20,16},{24,28},{28,24},{1,5},{5... | collective-permute-start | bytes 786440 | tf_op jit(solution)/shard_map/ppermute | solution.py:297
  22.9 1.6 %shard_map.76 = (f32[8,256]{1,0:T(8,128)S(1)}, f32[8,256]{1,0:T(8,128)S(1)}) custom-call(bf16[256,256]{1,0:T(8,128)(2,1)S(1)} %get-tuple-element.16.top, bf16[256,256]{1,0:T(8,128)(2,1)S(1)} %get-tuple-element.17.rest, f32[4,256,256]{2,1,0:T(8,128)S(1)} %get-tuple-element.18.maps, f32[8,256]{1,0:T(8,128)S(1)} %copy-done, ...), custom_call_target="tpu_custom_call" | custom-call | flops 1000000000 | bytes 2000000 | tf_op jit(solution)/shard_map/pallas_call | solution.py:34
  24.5 0.9 %collective-permute-start.6 = (f32[1,256]{1,0:T(1,128)S(1)}, f32[1,256]{1,0:T(1,128)S(1)}, u32[]{:S(2)}, u32[]{:S(2)}) collective-permute-start(f32[1,256]{1,0:T(1,128)S(1)} %slice.2), channel_id=1, source_target_pairs={{0,4},{4,0},{8,12},{12,8},{16,20},{20,16},{24,28},{28,24},{1,5},{5... | collective-permute-start | bytes 3080 | tf_op jit(solution)/shard_map/ppermute | solution.py:296
  25.4 2.7 %collective-permute-done.6 = f32[1,256]{1,0:T(1,128)S(1)} collective-permute-done((f32[1,256]{1,0:T(1,128)S(1)}, f32[1,256]{1,0:T(1,128)S(1)}, u32[]{:S(2)}, u32[]{:S(2)}) %collective-permute-start.6) | collective-permute-done | bytes 1056 | tf_op jit(solution)/shard_map/ppermute | solution.py:296
  28.5 3.3 %collective-permute-start.8 = (f32[1,256]{1,0:T(1,128)S(1)}, f32[1,256]{1,0:T(1,128)S(1)}, u32[]{:S(2)}, u32[]{:S(2)}) collective-permute-start(f32[1,256]{1,0:T(1,128)S(1)} %convolution_add_fusion.5), channel_id=1, source_target_pairs={{0,8},{4,12},{8,0},{12,4},{16,24},{20,28},{24,16},{28,20},{1,9},{5... | collective-permute-start | bytes 3080 | tf_op jit(solution)/shard_map/ppermute | solution.py:296
  32.5 0.9 %collective-permute-done.8 = f32[1,256]{1,0:T(1,128)S(1)} collective-permute-done((f32[1,256]{1,0:T(1,128)S(1)}, f32[1,256]{1,0:T(1,128)S(1)}, u32[]{:S(2)}, u32[]{:S(2)}) %collective-permute-start.8) | collective-permute-done | bytes 1056 | tf_op jit(solution)/shard_map/ppermute | solution.py:296
  33.5 10.5 %collective-permute-done.9 = f32[256,256]{1,0:T(8,128)S(1)} collective-permute-done((f32[256,256]{1,0:T(8,128)S(1)}, f32[256,256]{1,0:T(8,128)S(1)}, u32[]{:S(2)}, u32[]{:S(2)}) %collective-permute-start.9) | collective-permute-done | bytes 262176 | tf_op jit(solution)/shard_map/ppermute | solution.py:297
  44.2 3.7 %collective-permute-start.10 = (f32[1,256]{1,0:T(1,128)S(1)}, f32[1,256]{1,0:T(1,128)S(1)}, u32[]{:S(2)}, u32[]{:S(2)}) collective-permute-start(f32[1,256]{1,0:T(1,128)S(1)} %convolution_add_fusion.4), channel_id=1, source_target_pairs={{0,28},{4,24},{8,20},{12,16},{16,12},{20,8},{24,4},{28,0},{1,29},{... | collective-permute-start | bytes 3080 | tf_op jit(solution)/shard_map/ppermute | solution.py:296
  47.9 0.3 fusion.1
  48.6 0.9 %collective-permute-done.10 = f32[1,256]{1,0:T(1,128)S(1)} collective-permute-done((f32[1,256]{1,0:T(1,128)S(1)}, f32[1,256]{1,0:T(1,128)S(1)}, u32[]{:S(2)}, u32[]{:S(2)}) %collective-permute-start.10) | collective-permute-done | bytes 1056 | tf_op jit(solution)/shard_map/ppermute | solution.py:296
  49.6 12.5 %collective-permute-done.11 = f32[256,256]{1,0:T(8,128)S(1)} collective-permute-done((f32[256,256]{1,0:T(8,128)S(1)}, f32[256,256]{1,0:T(8,128)S(1)}, u32[]{:S(2)}, u32[]{:S(2)}) %collective-permute-start.11) | collective-permute-done | bytes 262176 | tf_op jit(solution)/shard_map/ppermute | solution.py:297
  62.3 0.3 fusion.2
  62.6 0.6 collective-permute-start.13
  63.7 0.7 collective-permute-done.13
  64.5 0.7 collective-permute-start.14
  65.2 0.3 fusion.3
  65.7 0.7 collective-permute-start.15
  66.6 1.3 %collective-permute-start.16 = (f32[1,256]{1,0:T(1,128)S(1)}, f32[1,256]{1,0:T(1,128)S(1)}, u32[]{:S(2)}, u32[]{:S(2)}) collective-permute-start(f32[1,256]{1,0:T(1,128)S(1)} %convolution_add_fusion), channel_id=1, source_target_pairs={{128,192},{129,193},{130,194},{131,195},{132,196},{133,197},{134,1... | collective-permute-start | bytes 3080 | tf_op jit(solution)/shard_map/ppermute | solution.py:310
  68.2 9.2 %collective-permute-done.16 = f32[1,256]{1,0:T(1,128)S(1)} collective-permute-done((f32[1,256]{1,0:T(1,128)S(1)}, f32[1,256]{1,0:T(1,128)S(1)}, u32[]{:S(2)}, u32[]{:S(2)}) %collective-permute-start.16) | collective-permute-done | bytes 1056 | tf_op jit(solution)/shard_map/ppermute | solution.py:310
  77.4 2.0 %shard_map.77 = f32[8,256]{1,0:T(8,128)} custom-call(bf16[256,256]{1,0:T(8,128)(2,1)S(1)} %get-tuple-element.16.top, bf16[256,256]{1,0:T(8,128)(2,1)S(1)} %get-tuple-element.17.rest, f32[8,256]{1,0:T(8,128)S(1)} %broadcast_in_dim.12.entry, f32[256,256]{1,0:T(8,128)S(1)} %convolution_select_fusion.own_map, f32[8,256]{1,0:T(8,128)S(1)} %add_select_fusion.own_entry, ...), custom_call_target="tpu_custom_call" | custom-call | flops 100000000 | bytes 1000000 | tf_op jit(solution)/shard_map/pallas_call | solution.py:34
  (52 shorter events, 4.1 us)
Async XLA Ops:
  0.0 16.7 %collective-permute-start.2 = (f32[8,256]{1,0:T(8,128)}, f32[8,256]{1,0:T(8,128)S(1)}, u32[]{:S(2)}, u32[]{:S(2)}) collective-permute-start(f32[8,256]{1,0:T(8,128)} %retain.3), channel_id=1, source_target_pairs={{0,3},{1,0},{2,1},{3,2},{4,7},{5,4},{6,5},{7,6},{8,11},{9,8},{10,9... | collective-permute-start | bytes 24584 | tf_op jit(solution)/shard_map/ppermute | solution.py:246
  3.0 14.0 %collective-permute-start.1 = (f32[8,256]{1,0:T(8,128)}, f32[8,256]{1,0:T(8,128)S(1)}, u32[]{:S(2)}, u32[]{:S(2)}) collective-permute-start(f32[8,256]{1,0:T(8,128)} %retain.3), channel_id=1, source_target_pairs={{0,2},{1,3},{2,0},{3,1},{4,6},{5,7},{6,4},{7,5},{8,10},{9,11},{10,... | collective-permute-start | bytes 24584 | tf_op jit(solution)/shard_map/ppermute | solution.py:246
  3.6 13.3 %collective-permute-start = (f32[8,256]{1,0:T(8,128)}, f32[8,256]{1,0:T(8,128)S(1)}, u32[]{:S(2)}, u32[]{:S(2)}) collective-permute-start(f32[8,256]{1,0:T(8,128)} %retain.3), channel_id=1, source_target_pairs={{0,1},{1,2},{2,3},{3,0},{4,5},{5,6},{6,7},{7,4},{8,9},{9,10},{10,1... | collective-permute-start | bytes 24584 | tf_op jit(solution)/shard_map/ppermute | solution.py:246
  5.5 1.2 %copy-start.1 = (bf16[4,4,128,256]{3,2,1,0:T(8,128)(2,1)S(1)}, bf16[4,4,128,256]{3,2,1,0:T(8,128)(2,1)}, u32[]{:S(2)}) copy-start(bf16[4,4,128,256]{3,2,1,0:T(8,128)(2,1)} %param.10) | copy-start | bytes 3145732
  5.9 0.8 copy-start
  6.0 1.0 %copy-start.2 = (bf16[8,64,192]{2,1,0:T(8,128)(2,1)S(1)}, bf16[8,64,192]{2,1,0:T(8,128)(2,1)}, u32[]{:S(2)}) copy-start(bf16[8,64,192]{2,1,0:T(8,128)(2,1)} %frames.1) | copy-start | bytes 589828
  6.0 1.1 %copy-start.3 = (bf16[4,4,64,128]{3,2,1,0:T(8,128)(2,1)S(1)}, bf16[4,4,64,128]{3,2,1,0:T(8,128)(2,1)}, u32[]{:S(2)}) copy-start(bf16[4,4,64,128]{3,2,1,0:T(8,128)(2,1)} %param.9) | copy-start | bytes 786436
  6.0 1.1 %copy-start.5 = (bf16[256,256]{1,0:T(8,128)(2,1)S(1)}, bf16[256,256]{1,0:T(8,128)(2,1)}, u32[]{:S(2)}) copy-start(bf16[256,256]{1,0:T(8,128)(2,1)} %observe.1) | copy-start | bytes 393220
  7.1 8.4 %copy-start.4 = (f32[256,256]{1,0:T(8,128)S(1)}, f32[256,256]{1,0:T(8,128)}, u32[]{:S(2)}) copy-start(f32[256,256]{1,0:T(8,128)} %source.1) | copy-start | bytes 786436
  11.6 11.3 %collective-permute-start.5 = (f32[8,256]{1,0:T(8,128)S(1)}, f32[8,256]{1,0:T(8,128)S(1)}, u32[]{:S(2)}, u32[]{:S(2)}) collective-permute-start(f32[8,256]{1,0:T(8,128)S(1)} %shard_map.74.refs_4_.drive), channel_id=1, source_target_pairs={{0,3},{1,0},{2,1},{3,2},{4,7},{5,4},{6,5},{7,6},{8,11},{9,8},{10,9... | collective-permute-start | bytes 24584 | tf_op jit(solution)/shard_map/ppermute | solution.py:246
  13.8 9.1 %collective-permute-start.4 = (f32[8,256]{1,0:T(8,128)S(1)}, f32[8,256]{1,0:T(8,128)S(1)}, u32[]{:S(2)}, u32[]{:S(2)}) collective-permute-start(f32[8,256]{1,0:T(8,128)S(1)} %shard_map.74.refs_4_.drive), channel_id=1, source_target_pairs={{0,2},{1,3},{2,0},{3,1},{4,6},{5,7},{6,4},{7,5},{8,10},{9,11},{10,... | collective-permute-start | bytes 24584 | tf_op jit(solution)/shard_map/ppermute | solution.py:246
  16.7 6.2 %collective-permute-start.3 = (f32[8,256]{1,0:T(8,128)S(1)}, f32[8,256]{1,0:T(8,128)S(1)}, u32[]{:S(2)}, u32[]{:S(2)}) collective-permute-start(f32[8,256]{1,0:T(8,128)S(1)} %shard_map.74.refs_4_.drive), channel_id=1, source_target_pairs={{0,1},{1,2},{2,3},{3,0},{4,5},{5,6},{6,7},{7,4},{8,9},{9,10},{10,1... | collective-permute-start | bytes 24584 | tf_op jit(solution)/shard_map/ppermute | solution.py:246
  20.9 7.4 %collective-permute-start.7 = (f32[256,256]{1,0:T(8,128)S(1)}, f32[256,256]{1,0:T(8,128)S(1)}, u32[]{:S(2)}, u32[]{:S(2)}) collective-permute-start(f32[256,256]{1,0:T(8,128)S(1)} %get-tuple-element.20), channel_id=1, source_target_pairs={{0,4},{4,0},{8,12},{12,8},{16,20},{20,16},{24,28},{28,24},{1,5},{5... | collective-permute-start | bytes 786440 | tf_op jit(solution)/shard_map/ppermute | solution.py:297
  24.5 3.6 %collective-permute-start.6 = (f32[1,256]{1,0:T(1,128)S(1)}, f32[1,256]{1,0:T(1,128)S(1)}, u32[]{:S(2)}, u32[]{:S(2)}) collective-permute-start(f32[1,256]{1,0:T(1,128)S(1)} %slice.2), channel_id=1, source_target_pairs={{0,4},{4,0},{8,12},{12,8},{16,20},{20,16},{24,28},{28,24},{1,5},{5... | collective-permute-start | bytes 3080 | tf_op jit(solution)/shard_map/ppermute | solution.py:296
  28.5 4.9 %collective-permute-start.8 = (f32[1,256]{1,0:T(1,128)S(1)}, f32[1,256]{1,0:T(1,128)S(1)}, u32[]{:S(2)}, u32[]{:S(2)}) collective-permute-start(f32[1,256]{1,0:T(1,128)S(1)} %convolution_add_fusion.5), channel_id=1, source_target_pairs={{0,8},{4,12},{8,0},{12,4},{16,24},{20,28},{24,16},{28,20},{1,9},{5... | collective-permute-start | bytes 3080 | tf_op jit(solution)/shard_map/ppermute | solution.py:296
  32.1 11.9 %collective-permute-start.9 = (f32[256,256]{1,0:T(8,128)S(1)}, f32[256,256]{1,0:T(8,128)S(1)}, u32[]{:S(2)}, u32[]{:S(2)}) collective-permute-start(f32[256,256]{1,0:T(8,128)S(1)} %fusion), channel_id=1, source_target_pairs={{0,8},{4,12},{8,0},{12,4},{16,24},{20,28},{24,16},{28,20},{1,9},{5... | collective-permute-start | bytes 786440 | tf_op jit(solution)/shard_map/ppermute | solution.py:297
  44.2 5.3 %collective-permute-start.10 = (f32[1,256]{1,0:T(1,128)S(1)}, f32[1,256]{1,0:T(1,128)S(1)}, u32[]{:S(2)}, u32[]{:S(2)}) collective-permute-start(f32[1,256]{1,0:T(1,128)S(1)} %convolution_add_fusion.4), channel_id=1, source_target_pairs={{0,28},{4,24},{8,20},{12,16},{16,12},{20,8},{24,4},{28,0},{1,29},{... | collective-permute-start | bytes 3080 | tf_op jit(solution)/shard_map/ppermute | solution.py:296
  48.2 13.9 %collective-permute-start.11 = (f32[256,256]{1,0:T(8,128)S(1)}, f32[256,256]{1,0:T(8,128)S(1)}, u32[]{:S(2)}, u32[]{:S(2)}) collective-permute-start(f32[256,256]{1,0:T(8,128)S(1)} %fusion.1), channel_id=1, source_target_pairs={{0,28},{4,24},{8,20},{12,16},{16,12},{20,8},{24,4},{28,0},{1,29},{... | collective-permute-start | bytes 786440 | tf_op jit(solution)/shard_map/ppermute | solution.py:297
  62.3 1.2 %collective-permute-start.12 = (f32[1,256]{1,0:T(1,128)S(1)}, f32[1,256]{1,0:T(1,128)S(1)}, u32[]{:S(2)}, u32[]{:S(2)}) collective-permute-start(f32[1,256]{1,0:T(1,128)S(1)} %convolution_add_fusion.3), channel_id=1, source_target_pairs={{0,32},{32,0},{1,33},{33,1},{2,34},{34,2},{3,35},{35,3},{4,36},{36... | collective-permute-start | bytes 3080 | tf_op jit(solution)/shard_map/ppermute | solution.py:296
  62.6 1.8 %collective-permute-start.13 = (f32[256,256]{1,0:T(8,128)S(1)}, f32[256,256]{1,0:T(8,128)S(1)}, u32[]{:S(2)}, u32[]{:S(2)}) collective-permute-start(f32[256,256]{1,0:T(8,128)S(1)} %fusion.2), channel_id=1, source_target_pairs={{0,32},{32,0},{1,33},{33,1},{2,34},{34,2},{3,35},{35,3},{4,36},{36... | collective-permute-start | bytes 786440 | tf_op jit(solution)/shard_map/ppermute | solution.py:297
  64.5 1.0 %collective-permute-start.14 = (f32[1,256]{1,0:T(1,128)S(1)}, f32[1,256]{1,0:T(1,128)S(1)}, u32[]{:S(2)}, u32[]{:S(2)}) collective-permute-start(f32[1,256]{1,0:T(1,128)S(1)} %convolution_add_fusion.2), channel_id=1, source_target_pairs={{0,64},{1,65},{2,66},{3,67},{4,68},{5,69},{6,70},{7,71},{8,72},{9,... | collective-permute-start | bytes 3080 | tf_op jit(solution)/shard_map/ppermute | solution.py:310
  65.7 0.7 collective-permute-start.15
  66.6 10.8 %collective-permute-start.16 = (f32[1,256]{1,0:T(1,128)S(1)}, f32[1,256]{1,0:T(1,128)S(1)}, u32[]{:S(2)}, u32[]{:S(2)}) collective-permute-start(f32[1,256]{1,0:T(1,128)S(1)} %convolution_add_fusion), channel_id=1, source_target_pairs={{128,192},{129,193},{130,194},{131,195},{132,196},{133,197},{134,1... | collective-permute-start | bytes 3080 | tf_op jit(solution)/shard_map/ppermute | solution.py:310

commit v2 on v1

v2 whole, which is shorter than its diff:
```python
import functools

import jax
import jax.numpy as jnp
import numpy as np
from jax import lax
from jax.experimental import pallas as pl
from jax.experimental.pallas import tpu as pltpu
from jax.sharding import Mesh, PartitionSpec as P

VMEM = pl.BlockSpec(memory_space=pltpu.VMEM)
LIMIT = 24 * 1024 * 1024
F32, BF16 = jnp.float32, jnp.bfloat16


def halves(value):
    top = value.astype(BF16)
    return top, (value - top.astype(F32)).astype(BF16)


def dot3(left, right):
    (left_top, left_rest), (right_top, right_rest) = left, right
    return (
        jnp.dot(left_top, right_rest, preferred_element_type=F32)
        + jnp.dot(left_rest, right_top, preferred_element_type=F32)
    ) + jnp.dot(left_top, right_top, preferred_element_type=F32)


def product(left, right):
    return dot3(halves(left), halves(right))


def call(kernel, outs, scratch, flops, traffic, *args):
    return pl.pallas_call(
        kernel,
        out_shape=[jax.ShapeDtypeStruct(shape, kind) for shape, kind in outs],
        in_specs=[VMEM] * len(args),
        out_specs=[VMEM] * len(outs),
        scratch_shapes=[pltpu.VMEM(shape, kind) for shape, kind in scratch],
        compiler_params=pltpu.CompilerParams(vmem_limit_bytes=LIMIT),
        cost_estimate=pl.CostEstimate(flops=flops, bytes_accessed=traffic, transcendentals=0),
    )(*args)


def rows_of(store, step, first, length):
    ways = store.shape[0]
    pieces = []
    for turn in range(ways // step):
        row = first + step * turn
        pieces.append(store[row % ways, pl.ds(row // ways, length * step // ways)])
    return pieces


def put_rows(store, value, first, start, size):
    ways = store.shape[0]
    share = value.shape[0] // ways
    for turn in range(ways):
        row = first + turn
        store[row % ways, pl.ds(row // ways, share), :, start : start + size] = value[turn * share : (turn + 1) * share]


def clear_rows(store, rows):
    for row in rows:
        store[row % store.shape[0], row // store.shape[0]] = jnp.zeros(store.shape[2:], F32)


def flatten(pieces, start, size):
    return jnp.concatenate([p[:, :, start : start + size].reshape(-1, size) for p in pieces], 0).astype(BF16)


def turn_of(source, factor):
    width = source.shape[0]
    skew = (source.T - source) * factor
    first = halves(skew)
    two = dot3(first, first)
    square = halves(two)
    three = dot3(first, square)
    four = dot3(square, square)
    row = lax.broadcasted_iota(jnp.int32, (width, width), 0)
    eye = (row == lax.broadcasted_iota(jnp.int32, (width, width), 1)).astype(F32)
    upper = eye / 24.0 + skew / 120.0 + two / 720.0 + three / 5040.0 + four / 40320.0
    return halves(skew + two / 2.0 + three / 6.0 + product(four, upper))


def encoder_kernel(factor, *refs):
    far, (raw, top, rest), near = refs[:7], refs[7:10], refs[10:17]
    flat, lines, wide, one, two, arrived = refs[17:]
    copies = [pltpu.make_async_copy(far[k], near[k], arrived.at[k]) for k in range(7)]
    for copy in copies[:3]:
        copy.start()
    source, frames, kernel, second, third, observe, retain = near
    count, height, row = frames.shape
    lanes = lines.shape[3]
    wide[...] = jnp.zeros_like(wide)
    clear_rows(lines, (0, height + 1))
    clear_rows(one, (0, height // 2 + 1))
    clear_rows(two, (0, height // 4 + 1))
    edge = jnp.zeros(two.shape[:3] + (128,), F32)
    two[:, :, :, :128] = edge
    two[:, :, :, two.shape[3] - 128 :] = edge
    for copy in copies[:3]:
        copy.wait()
    for copy in copies[3:]:
        copy.start()
    top[...], rest[...] = turn_of(source[...], factor)
    pixels = frames[...].astype(F32).reshape(count * height, row)
    pixels = jnp.concatenate([pixels, jnp.zeros((count * height, lanes - row), F32)], 1)
    pixels = pltpu.roll(pixels, 9, 1)
    flat[0] = pixels[:, :128]
    flat[1] = pixels[:, 128:]
    for h in range(height):
        for side in range(2):
            picked = flat[side, pl.ds(h, count, stride=height), :]
            lines[(h + 1) % 8, (h + 1) // 8, :, 128 * side : 128 * side + 128] = picked
    taps, depth, broad = kernel.shape[0], 64, wide.shape[2]
    room = lanes - depth
    for tap in range(taps):
        base = [kernel[tap, k].astype(F32) for k in range(taps)]
        base = jnp.concatenate(base + [jnp.zeros((depth - 12, 64), F32)], 0)
        band = jnp.concatenate([base] + [pltpu.roll(base, 6 * k, 0) for k in range(1, 8)], 1)
        wide[tap, room : room + depth, :] = band.astype(BF16)

    rows = height // 2
    sources = [flatten(rows_of(lines, 2, tap, rows), 0, lanes) for tap in range(taps)]
    halved = [[jnp.concatenate([p[:, k : k + 128] for p in sources[t : t + 2]], 1) for k in (0, 128)] for t in (0, 2)]
    total = one.shape[3]
    for start in range(0, total, broad):
        size = min(broad, total - start)
        shift = start // broad * 48
        value = None
        for side in range(2):
            if shift >= 128 * (side + 1) or shift + 54 <= 128 * side:
                continue
            first = room - shift + 128 * side
            for pair in range(2):
                weights = [wide[2 * pair + k, first : first + 128, :size] for k in range(2)]
                part = jnp.dot(halved[pair][side], jnp.concatenate(weights, 0), preferred_element_type=F32)
                value = part if value is None else value + part
        value = jnp.maximum(value, 0.0).astype(BF16).astype(F32)
        lane = lax.broadcasted_iota(jnp.int32, value.shape, 1) + start
        if start == 0:
            value = jnp.where(lane >= 64, value, 0.0)
        if start + size == total:
            value = jnp.where(lane < total - 64, value, 0.0)
        put_rows(one, value.reshape(rows, count, size), 1, start, size)

    copies[3].wait()
    rows = rows // 2
    weights = []
    for pair in range(2):
        taps_of = [second[2 * pair + k] for k in range(2)]
        sides = [jnp.concatenate([t[128 * side : 128 * side + 128] for t in taps_of], 0) for side in range(2)]
        weights.append(jnp.concatenate(sides, 1))
    left = None
    for tile in range(rows + 1):
        lanes_of = slice(128 * tile, 128 * tile + 128)
        value = None
        for pair in range(2):
            pieces = [flatten([p[:, :, lanes_of] for p in rows_of(one, 2, 2 * pair + k, rows)], 0, 128) for k in range(2)]
            part = jnp.dot(jnp.concatenate(pieces, 1), weights[pair], preferred_element_type=F32)
            value = part if value is None else value + part
        if tile > 0:
            result = jnp.maximum(left + value[:, 128:], 0.0).astype(BF16).astype(F32)
            put_rows(two, result.reshape(rows, count, 128), 1, 128 * tile, 128)
        left = value[:, :128]

    for copy in copies[4:]:
        copy.wait()
    rows = rows // 2
    value = jnp.zeros((rows * rows * count, third.shape[2]), F32)
    for tap in range(4):
        pieces = [flatten(rows_of(two, 2, tap, rows), 256 * j, 512) for j in range(rows)]
        value += jnp.dot(jnp.concatenate(pieces, 0), third[tap], preferred_element_type=F32)
    value = jnp.maximum(value, 0.0).reshape(rows * rows, count, value.shape[1])
    pooled = (jnp.sum(value, 0) * (1.0 / (rows * rows))).astype(BF16)
    raw[:count, :] = retain[...]
    raw[count:, :] = (1.0 - retain[...]) * jnp.dot(pooled, observe[...], preferred_element_type=F32)


def encode(factor, frames, conv_first, second_kernel_weight, conv_third, observe_map, skew_source, retain):
    count, height, row = frames.shape
    local, width = retain.shape
    far = [
        skew_source,
        frames,
        conv_first,
        second_kernel_weight.reshape(4, 256, 128),
        conv_third.reshape(4, 512, 256),
        observe_map,
        retain,
    ]
    outs = [((2 * local, width), F32), ((width, width), BF16), ((width, width), BF16)]
    scratch = [
        ((2, count * height, 128), F32),
        ((8, height // 8 + 1, count, 256), F32),
        ((4, 448, 512), BF16),
        ((4, height // 8 + 1, count, 34 * 64), F32),
        ((2, height // 8 + 1, count, 18 * 128), F32),
    ]
    return pl.pallas_call(
        functools.partial(encoder_kernel, factor),
        out_shape=[jax.ShapeDtypeStruct(shape, kind) for shape, kind in outs],
        in_specs=[pl.BlockSpec(memory_space=pltpu.HBM)] * len(far),
        out_specs=[VMEM] * len(outs),
        scratch_shapes=[pltpu.VMEM(a.shape, a.dtype) for a in far]
        + [pltpu.VMEM(shape, kind) for shape, kind in scratch]
        + [pltpu.SemaphoreType.DMA((len(far),))],
        compiler_params=pltpu.CompilerParams(vmem_limit_bytes=60 * 1024 * 1024),
        cost_estimate=pl.CostEstimate(flops=5 * 10**9, bytes_accessed=2 * 10**6, transcendentals=0),
    )(*far)


def maps_kernel(mine, top, rest, raw, *refs):
    refs, place = refs[:-1], refs[-1]
    groups, count, rows, width = place.shape
    local, spare = rows // 2, 16
    me = lax.axis_index("y")
    for group in range(groups):
        for slot in range(count):
            piece = raw[(group * count + slot) * rows : (group * count + slot + 1) * rows, :]
            place[group, pl.ds(lax.bitwise_xor(me, slot), 1)] = piece[None]
    turn = (top[...], rest[...])
    row = lax.broadcasted_iota(jnp.int32, (width, width), 0)
    eye = (row == lax.broadcasted_iota(jnp.int32, (width, width), 1)).astype(F32)
    start = eye + (turn[0].astype(F32) + turn[1].astype(F32))
    total = groups * count

    def line(block, step):
        return place[block // count, block % count, step : step + 1, :]

    def stack(step):
        lines = [line(block, step) for block in range(total)]
        return jnp.concatenate(lines + [jnp.zeros((spare - total, width), F32)], 0)

    values = [start * line(block, 0) for block in range(total)]
    states = stack(local)
    for step in range(1, local):
        both = jnp.concatenate([values[0], states], 0)
        both = both + dot3(halves(both), turn)
        states = both[width:] * stack(step) + stack(local + step)
        values[0] = both[:width] * line(0, step)
        for block in range(1, total):
            values[block] = (values[block] + dot3(halves(values[block]), turn)) * line(block, step)

    def spread(block):
        return jnp.broadcast_to(states[block : block + 1], (spare, width))

    for group in range(groups):
        before = jnp.concatenate([values[group * count], spread(group * count)], 0)
        prefix = jnp.concatenate([eye, jnp.zeros((spare, width), F32)], 0)
        for k in range(1, count):
            block = group * count + k
            if mine:
                prefix = jnp.where(me == k, before, prefix)
            later = product(before, values[block])
            before = jnp.concatenate([later[:width], later[width:] + spread(block)], 0)
        refs[0][group] = before[: width + 8]
        if mine:
            refs[1][...] = prefix[: width + 8]


def group_maps(mine, top, rest, raw, width):
    rows = raw.shape[0]
    groups = rows // 64
    outs = [((groups, width + 8, width), F32)] + [((width + 8, width), F32)] * mine
    scratch = [((groups, 4, 16, width), F32)]
    cost = 4 * 10**9 * groups
    return call(functools.partial(maps_kernel, mine), outs, scratch, cost, 2 * 10**6, top, rest, raw)


def ahead_kernel(top, rest, own, raw, maps_top, maps_rest, states):
    turn = (top[...], rest[...])
    width, local = own.shape[1], states.shape[0]
    value, state = own[:width, :], own[width:, :]
    for step in range(local):
        keep = raw[step : step + 1, :]
        value = (value + dot3(halves(value), turn)) * keep
        state = (state + dot3(halves(state), turn)) * keep + raw[local + step : local + step + 1, :]
        lanes = slice(step * width, (step + 1) * width)
        maps_top[:, lanes], maps_rest[:, lanes] = halves(value)
        states[step : step + 1, :] = state[0:1]


def final_kernel(entry, late, maps_top, maps_rest, states, out):
    width = states.shape[1]
    state = product(jnp.broadcast_to(entry[...], (8, width)), late[:width, :]) + late[width:, :]
    rows = dot3(halves(state), (maps_top[...], maps_rest[...]))
    for step in range(states.shape[0]):
        out[step : step + 1, :] = rows[0:1, step * width : (step + 1) * width] + states[step : step + 1, :]


def dot(a, b):
    return jnp.dot(a, b, precision=lax.Precision.HIGH, preferred_element_type=F32)


def exchange_pairs(bit, count):
    if 2 * bit == count:
        return [(i, count - 1 - i) for i in range(count)]
    return [(i, i ^ bit) for i in range(count)]


def join(low, high):
    width = low.shape[1]
    return dot(low, high[:width]) + jnp.concatenate([jnp.zeros((width, width), F32), high[width:]], 0)


def on_device(frames, conv_first, second_kernel_weight, conv_third, observe_map, skew_source, retain):
    local, width = retain.shape
    count_x, count_y, count_z = lax.axis_size("x"), lax.axis_size("y"), lax.axis_size("z")
    total_frames = local * count_x * count_y * count_z * lax.axis_size("core")
    me_x, me_z, me_core = lax.axis_index("x"), lax.axis_index("z"), lax.axis_index("core")
    factor = float(np.float32(0.7) / np.sqrt(np.float32(total_frames)))

    raw, top, rest = encode(
        factor, frames, conv_first, second_kernel_weight, conv_third, observe_map, skew_source, retain
    )
    pieces = [lax.ppermute(raw, "y", [(i, i ^ k) for i in range(count_y)]) for k in range(1, count_y)]
    rows = jnp.concatenate([raw] + pieces, 0)
    beside = lax.ppermute(rows, "z", exchange_pairs(1, count_z))
    group, own = group_maps(True, top, rest, rows, width)
    beside, group = lax.optimization_barrier((beside, group))
    across = lax.ppermute(jnp.concatenate([rows, beside], 0), "z", exchange_pairs(2, count_z))
    (other,) = group_maps(False, top, rest, beside, width)
    across, other = lax.optimization_barrier((across, other))
    (others,) = group_maps(False, top, rest, across, width)

    odd, second = (me_z & 1) > 0, (me_z & 2) > 0
    low, high = jnp.where(odd, other[0], group[0]), jnp.where(odd, group[0], other[0])
    own = jnp.where(odd, join(low, own), own)
    pair = join(low, high)
    low, high = jnp.where(odd, others[1], others[0]), jnp.where(odd, others[0], others[1])
    other_pair = join(low, high)
    low, high = jnp.where(second, other_pair, pair), jnp.where(second, pair, other_pair)
    own = jnp.where(second, join(low, own), own)
    block = join(low, high)

    other = lax.ppermute(block, "z", exchange_pairs(4, count_z))
    ahead = call(
        ahead_kernel,
        [((width, local * width), BF16)] * 2 + [((local, width), F32)],
        [],
        10**9,
        10**6,
        top,
        rest,
        own,
        raw,
    )
    other, *ahead = lax.optimization_barrier((other, *ahead))
    upper = (me_z & 4) > 0
    low_half = jnp.where(upper, other, block)
    block = join(low_half, jnp.where(upper, block, other))

    other = lax.ppermute(block, "core", exchange_pairs(1, 2))
    low_core, high_core = jnp.where(me_core > 0, other, block), jnp.where(me_core > 0, block, other)
    block_end = dot(low_core[width : width + 1], high_core[:width]) + high_core[width : width + 1]
    block_end, low_core = lax.optimization_barrier((block_end, low_core))

    first_end = lax.ppermute(block_end, "x", [(0, 1)])
    block = join(low_core, high_core)
    third = lax.ppermute(block, "x", [(2, 3)])
    still = jnp.concatenate([jnp.eye(width, dtype=F32), jnp.zeros((8, width), F32)], 0)
    late = join(jnp.where(me_core > 0, low_core, still), jnp.where(upper, low_half, still))
    leaving = dot(first_end, block[:width]) + block_end
    for_fourth = lax.ppermute(leaving, "x", [(1, 3)])
    for_third = lax.ppermute(leaving, "x", [(1, 2)])
    entry = dot(for_fourth, third[:width]) + third[width : width + 1]
    entry = jnp.where(me_x == 1, first_end, jnp.where(me_x == 2, for_third, entry))

    (filtered,) = call(
        final_kernel, [((local, width), F32)], [], 10**8, 10**6, entry, late, *ahead
    )
    return filtered


def solution(mesh):
    grp, seg = mesh.shape["grp"], mesh.shape["seg"]
    parts = Mesh(mesh.devices.reshape(grp // 2, 2, seg // 4, 4), ("x", "core", "z", "y"))
    whole = ("x", "core", "z", "y")
    placed = (P(whole), P(), P(), P(), P(), P(), P(whole))
    return jax.shard_map(on_device, mesh=parts, in_specs=placed, out_specs=P(whole), check_vma=False)
```

time: 79.6 us -> 67.8 us (0.85)
  waiting for transfers between devices: 37.5 us -> 19.2 us
  Pallas kernels: 13.1 us -> 24.1 us
  starting transfers between devices: 22.4 us -> 19.5 us
  local copies, waits for them, and re-layouts: 2.43 us -> 1.38 us
  matrix products: 3.73 us -> 2.7 us
    ppermute x17 -> x11, waiting for transfers between devices: 37.5 us -> 19.2 us  [the longest x1 5.94 us: on_device(): other = lax.ppermute(block, 'z', exchange_pairs(4, count_z))]
    pallas_call x0 -> x1, Pallas kernels: none -> 5.53 us  [encode(): pl.pallas_call(functools.partial(encoder_kernel, factor), out_shape=[jax....]
    pallas_call x5, Pallas kernels: 13.1 us -> 18.6 us  [call(): pl.pallas_call(kernel, out_shape=[jax.ShapeDtypeStruct(shape, kind) for s...]
    ppermute x17 -> x11, starting transfers between devices: 22.4 us -> 19.5 us  [the longest x1 5.19 us: on_device(): other = lax.ppermute(block, 'z', exchange_pairs(4, count_z))]
    dot_general x18 -> x11, matrix products: 3.73 us -> 2.7 us  [dot(): jnp.dot(a, b, precision=lax.Precision.HIGH, preferred_element_type=F32)]
    unnamed x20 -> x15, local copies, waits for them, and re-layouts: 1.73 us -> 1.35 us
  transfers between devices with their start and end apart: 17 -> 11, of which waited for: 7 -> 7; matrix products, arithmetic and copies ran while one was open for 6% -> 2% of each run, Pallas kernels for 14% -> 15%
where the time goes in v2:
time: 67.8 us; the launch traced here: 67.5 us
  Pallas kernels  24.1 us (36%)
  starting transfers between devices  19.5 us (29%)
  waiting for transfers between devices  19.2 us (28%)
  matrix products  2.7 us (4%)
  local copies, waits for them, and re-layouts  1.38 us (2%)
    pallas_call x5, Pallas kernels, call(): pl.pallas_call(kernel, out_shape=[jax.ShapeDtypeStruct(shape, kind) for s...  18.6 us
    ppermute x1, waiting for transfers between devices, on_device(): other = lax.ppermute(block, 'z', exchange_pairs(4, count_z))  5.94 us
    pallas_call x1, Pallas kernels, encode(): pl.pallas_call(functools.partial(encoder_kernel, factor), out_shape=[jax....  5.53 us
    ppermute x1, starting transfers between devices, on_device(): other = lax.ppermute(block, 'z', exchange_pairs(4, count_z))  5.19 us
    ppermute x1, waiting for transfers between devices, on_device(): for_fourth = lax.ppermute(leaving, 'x', [(1, 3)])  5.15 us
    ppermute x3, waiting for transfers between devices, on_device(): lax.ppermute(raw, 'y', [(i, i ^ k) for i in range(count_y)])  4.84 us
    ppermute x3, starting transfers between devices, on_device(): lax.ppermute(raw, 'y', [(i, i ^ k) for i in range(count_y)])  4.79 us
    ppermute x1, starting transfers between devices, on_device(): lax.ppermute(jnp.concatenate([rows, beside], 0), 'z', exchange_pairs(2, c...  3.54 us
  transfers between devices with their start and end apart: 11, of which 7 were waited for; matrix products, arithmetic and copies ran while one was open for 2% of the time, Pallas kernels for 15%

profile of v2, /device:TPU:6, one launch (start us, length us, event | category | flops | bytes accessed | tf_op | source)
XLA Modules:
  0.0 67.5 jit_solution(1672741847913029962)
XLA Ops:
  0.0 1.3 %copy.8.refs_2_ = bf16[4,4,3,64]{3,2,1,0:T(4,128)(2,1)} copy(bf16[4,4,3,64]{3,1,2,0:T(4,128)(2,1)} %param.8) | data formatting | bytes 12288 | tf_op args[1]
  1.3 5.5 %shard_map.73 = (f32[16,256]{1,0:T(8,128)}, bf16[256,256]{1,0:T(8,128)(2,1)}, bf16[256,256]{1,0:T(8,128)(2,1)}) custom-call(f32[256,256]{1,0:T(8,128)} %refs_0_.1, bf16[8,64,192]{2,1,0:T(8,128)(2,1)} %refs_1_.1, bf16[4,4,3,64]{3,2,1,0:T(4,128)(2,1)} %copy.8.refs_2_, bf16[4,256,128]{2,1,0:T(8,128)(2,1)} %bitcast.41, bf16[4,512,256]{2,1,0:T(8,128)(2,1)} %bitcast.40, ...), custom_call_target="tpu_custom_call" | custom-call | flops 5000000000 | bytes 2000000 | tf_op jit(solution)/shard_map/pallas_call | solution.py:200
  6.9 1.7 %collective-permute-start = (f32[16,256]{1,0:T(8,128)}, f32[16,256]{1,0:T(8,128)S(1)}, u32[]{:S(2)}, u32[]{:S(2)}) collective-permute-start(f32[16,256]{1,0:T(8,128)} %get-tuple-element.25.raw), channel_id=1, source_target_pairs={{0,1},{1,0},{2,3},{3,2},{4,5},{5,4},{6,7},{7,6},{8,9},{9,8},{10,11... | collective-permute-start | bytes 49160 | tf_op jit(solution)/shard_map/ppermute | solution.py:317
  8.5 2.9 %collective-permute-start.1 = (f32[16,256]{1,0:T(8,128)}, f32[16,256]{1,0:T(8,128)S(1)}, u32[]{:S(2)}, u32[]{:S(2)}) collective-permute-start(f32[16,256]{1,0:T(8,128)} %get-tuple-element.25.raw), channel_id=1, source_target_pairs={{0,2},{1,3},{2,0},{3,1},{4,6},{5,7},{6,4},{7,5},{8,10},{9,11},{10,... | collective-permute-start | bytes 49160 | tf_op jit(solution)/shard_map/ppermute | solution.py:317
  11.4 0.2 collective-permute-start.2
  11.7 2.2 %collective-permute-done.1 = f32[16,256]{1,0:T(8,128)S(1)} collective-permute-done((f32[16,256]{1,0:T(8,128)}, f32[16,256]{1,0:T(8,128)S(1)}, u32[]{:S(2)}, u32[]{:S(2)}) %collective-permute-start.1) | collective-permute-done | bytes 16416 | tf_op jit(solution)/shard_map/ppermute | solution.py:317
  14.0 2.6 %collective-permute-done.2 = f32[16,256]{1,0:T(8,128)S(1)} collective-permute-done((f32[16,256]{1,0:T(8,128)}, f32[16,256]{1,0:T(8,128)S(1)}, u32[]{:S(2)}, u32[]{:S(2)}) %collective-permute-start.2) | collective-permute-done | bytes 16416 | tf_op jit(solution)/shard_map/ppermute | solution.py:317
  16.6 1.9 %collective-permute-start.3 = (f32[64,256]{1,0:T(8,128)S(1)}, f32[64,256]{1,0:T(8,128)S(1)}, u32[]{:S(2)}, u32[]{:S(2)}) collective-permute-start(f32[64,256]{1,0:T(8,128)S(1)} %get-tuple-element.46.raw), channel_id=1, source_target_pairs={{0,4},{4,0},{8,12},{12,8},{16,20},{20,16},{24,28},{28,24},{1,5},{5... | collective-permute-start | bytes 196616 | tf_op jit(solution)/shard_map/ppermute | solution.py:319
  18.5 3.8 %shard_map.74 = (f32[1,264,256]{2,1,0:T(8,128)S(1)}, f32[264,256]{1,0:T(8,128)S(1)}) custom-call(bf16[256,256]{1,0:T(8,128)(2,1)S(1)} %copy-done.1, bf16[256,256]{1,0:T(8,128)(2,1)S(1)} %copy-done.2, f32[64,256]{1,0:T(8,128)S(1)} %get-tuple-element.46.raw), custom_call_target="tpu_custom_call" | custom-call | flops 4000000000 | bytes 2000000 | tf_op jit(solution)/shard_map/pallas_call | solution.py:34
  22.4 3.5 %collective-permute-start.4 = (f32[128,256]{1,0:T(8,128)S(1)}, f32[128,256]{1,0:T(8,128)S(1)}, u32[]{:S(2)}, u32[]{:S(2)}) collective-permute-start(f32[128,256]{1,0:T(8,128)S(1)} %constant_dynamic-update-slice_fusion.4), channel_id=1, source_target_pairs={{0,8},{4,12},{8,0},{12,4},{16,24},{20,28},{24,16},{28,20},{1,9},{5... | collective-permute-start | bytes 393224 | tf_op jit(solution)/shard_map/ppermute | solution.py:322
  25.9 3.8 %shard_map.75 = f32[1,264,256]{2,1,0:T(8,128)S(1)} custom-call(bf16[256,256]{1,0:T(8,128)(2,1)S(1)} %copy-done.1, bf16[256,256]{1,0:T(8,128)(2,1)S(1)} %copy-done.2, f32[64,256]{1,0:T(8,128)S(1)} %collective-permute-done.3.raw), custom_call_target="tpu_custom_call" | custom-call | flops 4000000000 | bytes 2000000 | tf_op jit(solution)/shard_map/pallas_call | solution.py:34
  29.7 0.2 collective-permute-done.4.raw
  29.9 0.3 fusion.1
  30.2 7.5 %shard_map.76 = f32[2,264,256]{2,1,0:T(8,128)S(1)} custom-call(bf16[256,256]{1,0:T(8,128)(2,1)S(1)} %copy-done.1, bf16[256,256]{1,0:T(8,128)(2,1)S(1)} %copy-done.2, f32[128,256]{1,0:T(8,128)S(1)} %collective-permute-done.4.raw), custom_call_target="tpu_custom_call" | custom-call | flops 8000000000 | bytes 2000000 | tf_op jit(solution)/shard_map/pallas_call | solution.py:34
  37.8 0.3 convolution_add_fusion.7
  38.1 0.3 broadcast_select_fusion.2
  38.5 0.3 convolution_add_fusion.5
  38.8 5.2 %collective-permute-start.5 = (f32[264,256]{1,0:T(8,128)S(1)}, f32[264,256]{1,0:T(8,128)S(1)}, u32[]{:S(2)}, u32[]{:S(2)}) collective-permute-start(f32[264,256]{1,0:T(8,128)S(1)} %convolution_add_fusion.5), channel_id=1, source_target_pairs={{0,28},{4,24},{8,20},{12,16},{16,12},{20,8},{24,4},{28,0},{1,29},{... | collective-permute-start | bytes 811016 | tf_op jit(solution)/shard_map/ppermute | solution.py:337
  44.0 0.3 fusion.own
  44.3 2.2 %shard_map.77 = (bf16[256,2048]{1,0:T(8,128)(2,1)S(1)}, bf16[256,2048]{1,0:T(8,128)(2,1)S(1)}, f32[8,256]{1,0:T(8,128)S(1)}) custom-call(bf16[256,256]{1,0:T(8,128)(2,1)S(1)} %copy-done.1, bf16[256,256]{1,0:T(8,128)(2,1)S(1)} %copy-done.2, f32[264,256]{1,0:T(8,128)S(1)} %fusion.own, f32[16,256]{1,0:T(8,128)S(1)} %copy-done), custom_call_target="tpu_custom_call" | custom-call | flops 1000000000 | bytes 1000000 | tf_op jit(solution)/shard_map/pallas_call | solution.py:34
  46.5 5.9 %collective-permute-done.5 = f32[264,256]{1,0:T(8,128)S(1)} collective-permute-done((f32[264,256]{1,0:T(8,128)S(1)}, f32[264,256]{1,0:T(8,128)S(1)}, u32[]{:S(2)}, u32[]{:S(2)}) %collective-permute-start.5) | collective-permute-done | bytes 270368 | tf_op jit(solution)/shard_map/ppermute | solution.py:337
  52.5 0.3 convolution_add_fusion.2
  52.9 1.5 %collective-permute-done.6 = f32[264,256]{1,0:T(8,128)S(1)} collective-permute-done((f32[264,256]{1,0:T(8,128)S(1)}, f32[264,256]{1,0:T(8,128)S(1)}, u32[]{:S(2)}, u32[]{:S(2)}) %collective-permute-start.6) | collective-permute-done | bytes 270368 | tf_op jit(solution)/shard_map/ppermute | solution.py:354
  54.6 0.7 %collective-permute-start.7 = (f32[1,256]{1,0:T(1,128)S(1)}, f32[1,256]{1,0:T(1,128)S(1)}, u32[]{:S(2)}, u32[]{:S(2)}) collective-permute-start(f32[1,256]{1,0:T(1,128)S(1)} %convolution_add_fusion.10), channel_id=1, source_target_pairs={{0,64},{1,65},{2,66},{3,67},{4,68},{5,69},{6,70},{7,71},{8,72},{9,... | collective-permute-start | bytes 3080 | tf_op jit(solution)/shard_map/ppermute | solution.py:359
  55.3 0.3 convolution_add_fusion.1
  55.6 1.3 %collective-permute-start.10 = (f32[264,256]{1,0:T(8,128)S(1)}, f32[264,256]{1,0:T(8,128)S(1)}, u32[]{:S(2)}, u32[]{:S(2)}) collective-permute-start(f32[264,256]{1,0:T(8,128)S(1)} %convolution_add_fusion.1), channel_id=1, source_target_pairs={{128,192},{129,193},{130,194},{131,195},{132,196},{133,197},{134,1... | collective-permute-start | bytes 811016 | tf_op jit(solution)/shard_map/ppermute | solution.py:361
  57.1 1.3 %collective-permute-start.9 = (f32[1,256]{1,0:T(1,128)S(1)}, f32[1,256]{1,0:T(1,128)S(1)}, u32[]{:S(2)}, u32[]{:S(2)}) collective-permute-start(f32[1,256]{1,0:T(1,128)S(1)} %convolution_add_fusion.9), channel_id=1, source_target_pairs={{64,192},{65,193},{66,194},{67,195},{68,196},{69,197},{70,198},{71... | collective-permute-start | bytes 3080 | tf_op jit(solution)/shard_map/ppermute | solution.py:365
  58.4 0.3 convolution_add_fusion.late
  58.7 0.7 collective-permute-start.8
  59.4 5.1 %collective-permute-done.9 = f32[1,256]{1,0:T(1,128)S(1)} collective-permute-done((f32[1,256]{1,0:T(1,128)S(1)}, f32[1,256]{1,0:T(1,128)S(1)}, u32[]{:S(2)}, u32[]{:S(2)}) %collective-permute-start.9) | collective-permute-done | bytes 1056 | tf_op jit(solution)/shard_map/ppermute | solution.py:365
  64.5 1.5 %collective-permute-done.10 = f32[264,256]{1,0:T(8,128)S(1)} collective-permute-done((f32[264,256]{1,0:T(8,128)S(1)}, f32[264,256]{1,0:T(8,128)S(1)}, u32[]{:S(2)}, u32[]{:S(2)}) %collective-permute-start.10) | collective-permute-done | bytes 270368 | tf_op jit(solution)/shard_map/ppermute | solution.py:361
  66.2 1.3 %shard_map.78 = f32[8,256]{1,0:T(8,128)} custom-call(f32[1,256]{1,0:T(1,128)S(1)} %broadcast_select_fusion.14.entry, f32[264,256]{1,0:T(8,128)S(1)} %convolution_add_fusion.late, bf16[256,2048]{1,0:T(8,128)(2,1)S(1)} %get-tuple-element.38.maps_top, bf16[256,2048]{1,0:T(8,128)(2,1)S(1)} %get-tuple-element.39.maps_rest, f32[8,256]{1,0:T(8,128)S(1)} %get-tuple-element.40.states), custom_call_target="tpu_custom_call" | custom-call | flops 100000000 | bytes 1000000 | tf_op jit(solution)/shard_map/pallas_call | solution.py:34
  (37 shorter events, 0.9 us)
Async XLA Ops:
  6.8 4.8 %copy-start = (f32[16,256]{1,0:T(8,128)S(1)}, f32[16,256]{1,0:T(8,128)}, u32[]{:S(2)}) copy-start(f32[16,256]{1,0:T(8,128)} %get-tuple-element.25.raw) | copy-start | bytes 49156
  6.9 4.9 %collective-permute-start = (f32[16,256]{1,0:T(8,128)}, f32[16,256]{1,0:T(8,128)S(1)}, u32[]{:S(2)}, u32[]{:S(2)}) collective-permute-start(f32[16,256]{1,0:T(8,128)} %get-tuple-element.25.raw), channel_id=1, source_target_pairs={{0,1},{1,0},{2,3},{3,2},{4,5},{5,4},{6,7},{7,6},{8,9},{9,8},{10,11... | collective-permute-start | bytes 49160 | tf_op jit(solution)/shard_map/ppermute | solution.py:317
  8.5 5.5 %collective-permute-start.1 = (f32[16,256]{1,0:T(8,128)}, f32[16,256]{1,0:T(8,128)S(1)}, u32[]{:S(2)}, u32[]{:S(2)}) collective-permute-start(f32[16,256]{1,0:T(8,128)} %get-tuple-element.25.raw), channel_id=1, source_target_pairs={{0,2},{1,3},{2,0},{3,1},{4,6},{5,7},{6,4},{7,5},{8,10},{9,11},{10,... | collective-permute-start | bytes 49160 | tf_op jit(solution)/shard_map/ppermute | solution.py:317
  11.4 5.2 %collective-permute-start.2 = (f32[16,256]{1,0:T(8,128)}, f32[16,256]{1,0:T(8,128)S(1)}, u32[]{:S(2)}, u32[]{:S(2)}) collective-permute-start(f32[16,256]{1,0:T(8,128)} %get-tuple-element.25.raw), channel_id=1, source_target_pairs={{0,3},{1,2},{2,1},{3,0},{4,7},{5,6},{6,5},{7,4},{8,11},{9,10},{10,... | collective-permute-start | bytes 49160 | tf_op jit(solution)/shard_map/ppermute | solution.py:317
  11.6 6.9 %copy-start.2 = (bf16[256,256]{1,0:T(8,128)(2,1)S(1)}, bf16[256,256]{1,0:T(8,128)(2,1)}, u32[]{:S(2)}) copy-start(bf16[256,256]{1,0:T(8,128)(2,1)} %get-tuple-element.24.rest) | copy-start | bytes 393220
  11.7 6.8 %copy-start.1 = (bf16[256,256]{1,0:T(8,128)(2,1)S(1)}, bf16[256,256]{1,0:T(8,128)(2,1)}, u32[]{:S(2)}) copy-start(bf16[256,256]{1,0:T(8,128)(2,1)} %get-tuple-element.23.top) | copy-start | bytes 393220
  16.6 5.8 %collective-permute-start.3 = (f32[64,256]{1,0:T(8,128)S(1)}, f32[64,256]{1,0:T(8,128)S(1)}, u32[]{:S(2)}, u32[]{:S(2)}) collective-permute-start(f32[64,256]{1,0:T(8,128)S(1)} %get-tuple-element.46.raw), channel_id=1, source_target_pairs={{0,4},{4,0},{8,12},{12,8},{16,20},{20,16},{24,28},{28,24},{1,5},{5... | collective-permute-start | bytes 196616 | tf_op jit(solution)/shard_map/ppermute | solution.py:319
  22.4 7.6 %collective-permute-start.4 = (f32[128,256]{1,0:T(8,128)S(1)}, f32[128,256]{1,0:T(8,128)S(1)}, u32[]{:S(2)}, u32[]{:S(2)}) collective-permute-start(f32[128,256]{1,0:T(8,128)S(1)} %constant_dynamic-update-slice_fusion.4), channel_id=1, source_target_pairs={{0,8},{4,12},{8,0},{12,4},{16,24},{20,28},{24,16},{28,20},{1,9},{5... | collective-permute-start | bytes 393224 | tf_op jit(solution)/shard_map/ppermute | solution.py:322
  30.2 7.5 %copy-start.3 = (f32[264,256]{1,0:T(8,128)}, f32[264,256]{1,0:T(8,128)S(1)}, u32[]{:S(2)}) copy-start(f32[264,256]{1,0:T(8,128)S(1)} %fusion.1) | copy-start | bytes 811012
  38.4 5.5 %copy-start.4 = (f32[264,256]{1,0:T(8,128)S(1)}, f32[264,256]{1,0:T(8,128)}, u32[]{:S(2)}) copy-start(f32[264,256]{1,0:T(8,128)} %copy-done.3) | copy-start | bytes 811012
  38.5 5.5 %slice-start = ((f32[264,256]{1,0:T(8,128)}), f32[8,256]{1,0:T(8,128)S(1)}, s32[]{:S(2)}) async-start(f32[264,256]{1,0:T(8,128)} %copy-done.3), calls=%async_computation | async-start | bytes 16384 | tf_op jit(solution)/shard_map/slice | solution.py:304
  38.8 13.7 %collective-permute-start.5 = (f32[264,256]{1,0:T(8,128)S(1)}, f32[264,256]{1,0:T(8,128)S(1)}, u32[]{:S(2)}, u32[]{:S(2)}) collective-permute-start(f32[264,256]{1,0:T(8,128)S(1)} %convolution_add_fusion.5), channel_id=1, source_target_pairs={{0,28},{4,24},{8,20},{12,16},{16,12},{20,8},{24,4},{28,0},{1,29},{... | collective-permute-start | bytes 811016 | tf_op jit(solution)/shard_map/ppermute | solution.py:337
  52.8 1.6 %collective-permute-start.6 = (f32[264,256]{1,0:T(8,128)S(1)}, f32[264,256]{1,0:T(8,128)S(1)}, u32[]{:S(2)}, u32[]{:S(2)}) collective-permute-start(f32[264,256]{1,0:T(8,128)S(1)} %convolution_add_fusion.2), channel_id=1, source_target_pairs={{0,32},{32,0},{1,33},{33,1},{2,34},{34,2},{3,35},{35,3},{4,36},{36... | collective-permute-start | bytes 811016 | tf_op jit(solution)/shard_map/ppermute | solution.py:354
  54.6 2.3 %collective-permute-start.7 = (f32[1,256]{1,0:T(1,128)S(1)}, f32[1,256]{1,0:T(1,128)S(1)}, u32[]{:S(2)}, u32[]{:S(2)}) collective-permute-start(f32[1,256]{1,0:T(1,128)S(1)} %convolution_add_fusion.10), channel_id=1, source_target_pairs={{0,64},{1,65},{2,66},{3,67},{4,68},{5,69},{6,70},{7,71},{8,72},{9,... | collective-permute-start | bytes 3080 | tf_op jit(solution)/shard_map/ppermute | solution.py:359
  55.6 10.4 %collective-permute-start.10 = (f32[264,256]{1,0:T(8,128)S(1)}, f32[264,256]{1,0:T(8,128)S(1)}, u32[]{:S(2)}, u32[]{:S(2)}) collective-permute-start(f32[264,256]{1,0:T(8,128)S(1)} %convolution_add_fusion.1), channel_id=1, source_target_pairs={{128,192},{129,193},{130,194},{131,195},{132,196},{133,197},{134,1... | collective-permute-start | bytes 811016 | tf_op jit(solution)/shard_map/ppermute | solution.py:361
  57.1 7.4 %collective-permute-start.9 = (f32[1,256]{1,0:T(1,128)S(1)}, f32[1,256]{1,0:T(1,128)S(1)}, u32[]{:S(2)}, u32[]{:S(2)}) collective-permute-start(f32[1,256]{1,0:T(1,128)S(1)} %convolution_add_fusion.9), channel_id=1, source_target_pairs={{64,192},{65,193},{66,194},{67,195},{68,196},{69,197},{70,198},{71... | collective-permute-start | bytes 3080 | tf_op jit(solution)/shard_map/ppermute | solution.py:365
  58.7 7.5 %collective-permute-start.8 = (f32[1,256]{1,0:T(1,128)S(1)}, f32[1,256]{1,0:T(1,128)S(1)}, u32[]{:S(2)}, u32[]{:S(2)}) collective-permute-start(f32[1,256]{1,0:T(1,128)S(1)} %convolution_add_fusion.9), channel_id=1, source_target_pairs={{64,128},{65,129},{66,130},{67,131},{68,132},{69,133},{70,134},{71... | collective-permute-start | bytes 3080 | tf_op jit(solution)/shard_map/ppermute | solution.py:366

commit v3 on v2

--- a/solution.py
+++ b/solution.py
@@ -68,9 +68,9 @@
     return jnp.concatenate([p[:, :, start : start + size].reshape(-1, size) for p in pieces], 0).astype(BF16)
 
 
-def turn_of(source, factor):
+def turn_kernel(factor, source, top, rest):
     width = source.shape[0]
-    skew = (source.T - source) * factor
+    skew = (source[...].T - source[...]) * factor
     first = halves(skew)
     two = dot3(first, first)
     square = halves(two)
@@ -79,16 +79,16 @@
     row = lax.broadcasted_iota(jnp.int32, (width, width), 0)
     eye = (row == lax.broadcasted_iota(jnp.int32, (width, width), 1)).astype(F32)
     upper = eye / 24.0 + skew / 120.0 + two / 720.0 + three / 5040.0 + four / 40320.0
-    return halves(skew + two / 2.0 + three / 6.0 + product(four, upper))
-
-
-def encoder_kernel(factor, *refs):
-    far, (raw, top, rest), near = refs[:7], refs[7:10], refs[10:17]
-    flat, lines, wide, one, two, arrived = refs[17:]
-    copies = [pltpu.make_async_copy(far[k], near[k], arrived.at[k]) for k in range(7)]
-    for copy in copies[:3]:
+    top[...], rest[...] = halves(skew + two / 2.0 + three / 6.0 + product(four, upper))
+
+
+def encoder_kernel(*refs):
+    far, raw, near = refs[:6], refs[6], refs[7:13]
+    flat, lines, wide, one, two, arrived = refs[13:]
+    copies = [pltpu.make_async_copy(far[k], near[k], arrived.at[k]) for k in range(6)]
+    for copy in copies[:2]:
         copy.start()
-    source, frames, kernel, second, third, observe, retain = near
+    frames, kernel, second, third, observe, retain = near
     count, height, row = frames.shape
     lanes = lines.shape[3]
     wide[...] = jnp.zeros_like(wide)
@@ -98,11 +98,10 @@
     edge = jnp.zeros(two.shape[:3] + (128,), F32)
     two[:, :, :, :128] = edge
     two[:, :, :, two.shape[3] - 128 :] = edge
-    for copy in copies[:3]:
+    for copy in copies[:2]:
         copy.wait()
-    for copy in copies[3:]:
+    for copy in copies[2:]:
         copy.start()
-    top[...], rest[...] = turn_of(source[...], factor)
     pixels = frames[...].astype(F32).reshape(count * height, row)
     pixels = jnp.concatenate([pixels, jnp.zeros((count * height, lanes - row), F32)], 1)
     pixels = pltpu.roll(pixels, 9, 1)
@@ -115,7 +114,8 @@
     taps, depth, broad = kernel.shape[0], 64, wide.shape[2]
     room = lanes - depth
     for tap in range(taps):
-        base = [kernel[tap, k].astype(F32) for k in range(taps)]
+        colours = [kernel[tap, c].astype(F32) for c in range(3)]
+        base = [colours[c][k : k + 1] for k in range(taps) for c in range(3)]
         base = jnp.concatenate(base + [jnp.zeros((depth - 12, 64), F32)], 0)
         band = jnp.concatenate([base] + [pltpu.roll(base, 6 * k, 0) for k in range(1, 8)], 1)
         wide[tap, room : room + depth, :] = band.astype(BF16)
@@ -144,7 +144,7 @@
             value = jnp.where(lane < total - 64, value, 0.0)
         put_rows(one, value.reshape(rows, count, size), 1, start, size)
 
-    copies[3].wait()
+    copies[2].wait()
     rows = rows // 2
     weights = []
     for pair in range(2):
@@ -164,7 +164,7 @@
             put_rows(two, result.reshape(rows, count, 128), 1, 128 * tile, 128)
         left = value[:, :128]
 
-    for copy in copies[4:]:
+    for copy in copies[3:]:
         copy.wait()
     rows = rows // 2
     value = jnp.zeros((rows * rows * count, third.shape[2]), F32)
@@ -177,19 +177,17 @@
     raw[count:, :] = (1.0 - retain[...]) * jnp.dot(pooled, observe[...], preferred_element_type=F32)
 
 
-def encode(factor, frames, conv_first, second_kernel_weight, conv_third, observe_map, skew_source, retain):
+def encode(frames, conv_first, second_kernel_weight, conv_third, observe_map, retain):
     count, height, row = frames.shape
     local, width = retain.shape
     far = [
-        skew_source,
         frames,
-        conv_first,
+        jnp.transpose(conv_first, (0, 2, 1, 3)),
         second_kernel_weight.reshape(4, 256, 128),
         conv_third.reshape(4, 512, 256),
         observe_map,
         retain,
     ]
-    outs = [((2 * local, width), F32), ((width, width), BF16), ((width, width), BF16)]
     scratch = [
         ((2, count * height, 128), F32),
         ((8, height // 8 + 1, count, 256), F32),
@@ -198,10 +196,10 @@
         ((2, height // 8 + 1, count, 18 * 128), F32),
     ]
     return pl.pallas_call(
-        functools.partial(encoder_kernel, factor),
-        out_shape=[jax.ShapeDtypeStruct(shape, kind) for shape, kind in outs],
+        encoder_kernel,
+        out_shape=jax.ShapeDtypeStruct((2 * local, width), F32),
         in_specs=[pl.BlockSpec(memory_space=pltpu.HBM)] * len(far),
-        out_specs=[VMEM] * len(outs),
+        out_specs=VMEM,
         scratch_shapes=[pltpu.VMEM(a.shape, a.dtype) for a in far]
         + [pltpu.VMEM(shape, kind) for shape, kind in scratch]
         + [pltpu.SemaphoreType.DMA((len(far),))],
@@ -213,6 +211,8 @@
 def maps_kernel(mine, top, rest, raw, *refs):
     refs, place = refs[:-1], refs[-1]
     groups, count, rows, width = place.shape
+    known = refs[0] if groups == 2 else None
+    refs = refs[1:] if groups == 2 else refs
     local, spare = rows // 2, 16
     me = lax.axis_index("y")
     for group in range(groups):
@@ -245,6 +245,7 @@
     def spread(block):
         return jnp.broadcast_to(states[block : block + 1], (spare, width))
 
+    results = []
     for group in range(groups):
         before = jnp.concatenate([values[group * count], spread(group * count)], 0)
         prefix = jnp.concatenate([eye, jnp.zeros((spare, width), F32)], 0)
@@ -254,18 +255,31 @@
                 prefix = jnp.where(me == k, before, prefix)
             later = product(before, values[block])
             before = jnp.concatenate([later[:width], later[width:] + spread(block)], 0)
-        refs[0][group] = before[: width + 8]
+        results.append(before)
         if mine:
             refs[1][...] = prefix[: width + 8]
-
-
-def group_maps(mine, top, rest, raw, width):
-    rows = raw.shape[0]
-    groups = rows // 64
-    outs = [((groups, width + 8, width), F32)] + [((width + 8, width), F32)] * mine
+    if groups == 1:
+        refs[0][...] = results[0][: width + 8]
+        return
+
+    def joined(first, later):
+        result = product(first, later[:width])
+        return jnp.concatenate([result[:width], result[width:] + later[width:]], 0)
+
+    z = lax.axis_index("z")
+    odd, second = lax.rem(z, 2) == 1, lax.rem(z, 4) >= 2
+    pair = joined(*(jnp.where(odd, results[1 - k], results[k]) for k in range(2)))
+    known = jnp.concatenate([known[...], known[width:, :]], 0)
+    refs[0][...] = joined(jnp.where(second, pair, known), jnp.where(second, known, pair))[: width + 8]
+    refs[1][...] = pair[: width + 8]
+
+
+def group_maps(mine, top, rest, raw, *known):
+    width, groups = raw.shape[1], raw.shape[0] // 64
+    outs = [((width + 8, width), F32)] * (2 if mine or known else 1)
     scratch = [((groups, 4, 16, width), F32)]
     cost = 4 * 10**9 * groups
-    return call(functools.partial(maps_kernel, mine), outs, scratch, cost, 2 * 10**6, top, rest, raw)
+    return call(functools.partial(maps_kernel, mine), outs, scratch, cost, 2 * 10**6, top, rest, raw, *known)
 
 
 def ahead_kernel(top, rest, own, raw, maps_top, maps_rest, states):
@@ -311,30 +325,27 @@
     me_x, me_z, me_core = lax.axis_index("x"), lax.axis_index("z"), lax.axis_index("core")
     factor = float(np.float32(0.7) / np.sqrt(np.float32(total_frames)))
 
-    raw, top, rest = encode(
-        factor, frames, conv_first, second_kernel_weight, conv_third, observe_map, skew_source, retain
-    )
+    raw = encode(frames, conv_first, second_kernel_weight, conv_third, observe_map, retain)
+    skew_source, raw = lax.optimization_barrier((skew_source, raw))
+    square = ((width, width), BF16)
+    top, rest = call(functools.partial(turn_kernel, factor), [square] * 2, [], 10**9, 10**6, skew_source)
     pieces = [lax.ppermute(raw, "y", [(i, i ^ k) for i in range(count_y)]) for k in range(1, count_y)]
     rows = jnp.concatenate([raw] + pieces, 0)
     beside = lax.ppermute(rows, "z", exchange_pairs(1, count_z))
-    group, own = group_maps(True, top, rest, rows, width)
+    group, own = group_maps(True, top, rest, rows)
     beside, group = lax.optimization_barrier((beside, group))
     across = lax.ppermute(jnp.concatenate([rows, beside], 0), "z", exchange_pairs(2, count_z))
-    (other,) = group_maps(False, top, rest, beside, width)
+    (other,) = group_maps(False, top, rest, beside)
     across, other = lax.optimization_barrier((across, other))
-    (others,) = group_maps(False, top, rest, across, width)
 
     odd, second = (me_z & 1) > 0, (me_z & 2) > 0
-    low, high = jnp.where(odd, other[0], group[0]), jnp.where(odd, group[0], other[0])
+    low, high = jnp.where(odd, other, group), jnp.where(odd, group, other)
+    pair = join(low, high)
+    block, other_pair = group_maps(False, top, rest, across, pair)
     own = jnp.where(odd, join(low, own), own)
-    pair = join(low, high)
-    low, high = jnp.where(odd, others[1], others[0]), jnp.where(odd, others[0], others[1])
-    other_pair = join(low, high)
-    low, high = jnp.where(second, other_pair, pair), jnp.where(second, pair, other_pair)
-    own = jnp.where(second, join(low, own), own)
-    block = join(low, high)
 
     other = lax.ppermute(block, "z", exchange_pairs(4, count_z))
+    own = jnp.where(second, join(other_pair, own), own)
     ahead = call(
         ahead_kernel,
         [((width, local * width), BF16)] * 2 + [((local, width), F32)],
@@ -361,10 +372,12 @@
     third = lax.ppermute(block, "x", [(2, 3)])
     still = jnp.concatenate([jnp.eye(width, dtype=F32), jnp.zeros((8, width), F32)], 0)
     late = join(jnp.where(me_core > 0, low_core, still), jnp.where(upper, low_half, still))
+    first_end, late = lax.optimization_barrier((first_end, late))
     leaving = dot(first_end, block[:width]) + block_end
     for_fourth = lax.ppermute(leaving, "x", [(1, 3)])
     for_third = lax.ppermute(leaving, "x", [(1, 2)])
     entry = dot(for_fourth, third[:width]) + third[width : width + 1]
+    for_third, entry = lax.optimization_barrier((for_third, entry))
     entry = jnp.where(me_x == 1, first_end, jnp.where(me_x == 2, for_third, entry))
 
     (filtered,) = call(

time: 67.8 us -> 65 us (0.959)
  waiting for transfers between devices: 19.2 us -> 17.7 us
  local copies, waits for them, and re-layouts: 1.38 us -> 0.05 us
  Pallas kernels: 24.1 us -> 25 us
    pallas_call x5 -> x6, Pallas kernels: 18.6 us -> 20.4 us  [call(): pl.pallas_call(kernel, out_shape=[jax.ShapeDtypeStruct(shape, kind) for s...]
    unnamed x15 -> x7, local copies, waits for them, and re-layouts: 1.35 us -> 0.02 us
    ppermute x3, waiting for transfers between devices: 4.84 us -> 3.68 us  [on_device(): lax.ppermute(raw, 'y', [(i, i ^ k) for i in range(count_y)])]
    pallas_call x1, Pallas kernels: 5.53 us -> 4.5 us  [encode(): pl.pallas_call(encoder_kernel, out_shape=jax.ShapeDtypeStruct((2 * local,...]
    dot_general x11 -> x9, matrix products: 2.7 us -> 2.14 us  [dot(): jnp.dot(a, b, precision=lax.Precision.HIGH, preferred_element_type=F32)]
  transfers between devices with their start and end apart: 11 -> 11, of which waited for: 7 -> 7; matrix products, arithmetic and copies ran while one was open for 2% -> 2% of each run, Pallas kernels for 15% -> 17%
where the time goes in v3:
time: 65 us; the launch traced here: 64.9 us
  Pallas kernels  25 us (38%)
  starting transfers between devices  19.5 us (30%)
  waiting for transfers between devices  17.7 us (27%)
  matrix products  2.14 us (3%)
    pallas_call x6, Pallas kernels, call(): pl.pallas_call(kernel, out_shape=[jax.ShapeDtypeStruct(shape, kind) for s...  20.4 us
    ppermute x1, waiting for transfers between devices, on_device(): other = lax.ppermute(block, 'z', exchange_pairs(4, count_z))  5.64 us
    ppermute x1, starting transfers between devices, on_device(): other = lax.ppermute(block, 'z', exchange_pairs(4, count_z))  5.21 us
    ppermute x1, waiting for transfers between devices, on_device(): for_fourth = lax.ppermute(leaving, 'x', [(1, 3)])  5.16 us
    ppermute x3, starting transfers between devices, on_device(): lax.ppermute(raw, 'y', [(i, i ^ k) for i in range(count_y)])  4.79 us
    pallas_call x1, Pallas kernels, encode(): pl.pallas_call(encoder_kernel, out_shape=jax.ShapeDtypeStruct((2 * local,...  4.5 us
    ppermute x3, waiting for transfers between devices, on_device(): lax.ppermute(raw, 'y', [(i, i ^ k) for i in range(count_y)])  3.68 us
    ppermute x1, starting transfers between devices, on_device(): lax.ppermute(jnp.concatenate([rows, beside], 0), 'z', exchange_pairs(2, c...  3.54 us
  transfers between devices with their start and end apart: 11, of which 7 were waited for; matrix products, arithmetic and copies ran while one was open for 2% of the time, Pallas kernels for 17%

profile of v3, /device:TPU:6, one launch (start us, length us, event | category | flops | bytes accessed | tf_op | source)
XLA Modules:
  0.0 64.9 jit_solution(16121530427448004897)
XLA Ops:
  0.0 4.5 %shard_map.73.raw = f32[16,256]{1,0:T(8,128)} custom-call(bf16[8,64,192]{2,1,0:T(8,128)(2,1)} %refs_0_.1, bf16[4,3,4,64]{3,2,1,0:T(4,128)(2,1)} %bitcast.22, bf16[4,256,128]{2,1,0:T(8,128)(2,1)} %bitcast.21, bf16[4,512,256]{2,1,0:T(8,128)(2,1)} %bitcast.20, bf16[256,256]{1,0:T(8,128)(2,1)} %refs_4_.1, f32[8,256]{1,0:T(8,128)} %refs_5_.1), custom_call_target="tpu_custom_call" | custom-call | flops 5000000000 | bytes 2000000 | tf_op jit(solution)/shard_map/pallas_call | solution.py:198
  4.5 1.7 %collective-permute-start = (f32[16,256]{1,0:T(8,128)}, f32[16,256]{1,0:T(8,128)S(1)}, u32[]{:S(2)}, u32[]{:S(2)}) collective-permute-start(f32[16,256]{1,0:T(8,128)} %shard_map.73.raw), channel_id=1, source_target_pairs={{0,1},{1,0},{2,3},{3,2},{4,5},{5,4},{6,7},{7,6},{8,9},{9,8},{10,11... | collective-permute-start | bytes 49160 | tf_op jit(solution)/shard_map/ppermute | solution.py:332
  6.2 2.9 %collective-permute-start.1 = (f32[16,256]{1,0:T(8,128)}, f32[16,256]{1,0:T(8,128)S(1)}, u32[]{:S(2)}, u32[]{:S(2)}) collective-permute-start(f32[16,256]{1,0:T(8,128)} %shard_map.73.raw), channel_id=1, source_target_pairs={{0,2},{1,3},{2,0},{3,1},{4,6},{5,7},{6,4},{7,5},{8,10},{9,11},{10,... | collective-permute-start | bytes 49160 | tf_op jit(solution)/shard_map/ppermute | solution.py:332
  9.1 0.2 collective-permute-start.2
  9.4 1.2 %shard_map.74 = (bf16[256,256]{1,0:T(8,128)(2,1)S(1)}, bf16[256,256]{1,0:T(8,128)(2,1)S(1)}) custom-call(f32[256,256]{1,0:T(8,128)S(1)} %copy-done.1), custom_call_target="tpu_custom_call" | custom-call | flops 1000000000 | bytes 1000000 | tf_op jit(solution)/shard_map/pallas_call | solution.py:34
  10.6 1.1 %collective-permute-done.1 = f32[16,256]{1,0:T(8,128)S(1)} collective-permute-done((f32[16,256]{1,0:T(8,128)}, f32[16,256]{1,0:T(8,128)S(1)}, u32[]{:S(2)}, u32[]{:S(2)}) %collective-permute-start.1) | collective-permute-done | bytes 16416 | tf_op jit(solution)/shard_map/ppermute | solution.py:332
  11.6 2.6 %collective-permute-done.2 = f32[16,256]{1,0:T(8,128)S(1)} collective-permute-done((f32[16,256]{1,0:T(8,128)}, f32[16,256]{1,0:T(8,128)S(1)}, u32[]{:S(2)}, u32[]{:S(2)}) %collective-permute-start.2) | collective-permute-done | bytes 16416 | tf_op jit(solution)/shard_map/ppermute | solution.py:332
  14.3 1.9 %collective-permute-start.3 = (f32[64,256]{1,0:T(8,128)S(1)}, f32[64,256]{1,0:T(8,128)S(1)}, u32[]{:S(2)}, u32[]{:S(2)}) collective-permute-start(f32[64,256]{1,0:T(8,128)S(1)} %get-tuple-element.59.raw), channel_id=1, source_target_pairs={{0,4},{4,0},{8,12},{12,8},{16,20},{20,16},{24,28},{28,24},{1,5},{5... | collective-permute-start | bytes 196616 | tf_op jit(solution)/shard_map/ppermute | solution.py:334
  16.2 3.8 %shard_map.75 = (f32[264,256]{1,0:T(8,128)S(1)}, f32[264,256]{1,0:T(8,128)S(1)}) custom-call(bf16[256,256]{1,0:T(8,128)(2,1)S(1)} %get-tuple-element.31.top, bf16[256,256]{1,0:T(8,128)(2,1)S(1)} %get-tuple-element.32.rest, f32[64,256]{1,0:T(8,128)S(1)} %get-tuple-element.59.raw), custom_call_target="tpu_custom_call" | custom-call | flops 4000000000 | bytes 2000000 | tf_op jit(solution)/shard_map/pallas_call | solution.py:34
  20.0 3.5 %collective-permute-start.4 = (f32[128,256]{1,0:T(8,128)S(1)}, f32[128,256]{1,0:T(8,128)S(1)}, u32[]{:S(2)}, u32[]{:S(2)}) collective-permute-start(f32[128,256]{1,0:T(8,128)S(1)} %constant_dynamic-update-slice_fusion.4), channel_id=1, source_target_pairs={{0,8},{4,12},{8,0},{12,4},{16,24},{20,28},{24,16},{28,20},{1,9},{5... | collective-permute-start | bytes 393224 | tf_op jit(solution)/shard_map/ppermute | solution.py:337
  23.6 3.8 %shard_map.76 = f32[264,256]{1,0:T(8,128)S(1)} custom-call(bf16[256,256]{1,0:T(8,128)(2,1)S(1)} %get-tuple-element.31.top, bf16[256,256]{1,0:T(8,128)(2,1)S(1)} %get-tuple-element.32.rest, f32[64,256]{1,0:T(8,128)S(1)} %collective-permute-done.3.raw), custom_call_target="tpu_custom_call" | custom-call | flops 4000000000 | bytes 2000000 | tf_op jit(solution)/shard_map/pallas_call | solution.py:34
  27.4 0.2 collective-permute-done.4.raw
  27.6 0.3 convolution_add_fusion.5.refs_0_
  27.9 8.2 %shard_map.77 = (f32[264,256]{1,0:T(8,128)S(1)}, f32[264,256]{1,0:T(8,128)S(1)}) custom-call(bf16[256,256]{1,0:T(8,128)(2,1)S(1)} %get-tuple-element.31.top, bf16[256,256]{1,0:T(8,128)(2,1)S(1)} %get-tuple-element.32.rest, f32[128,256]{1,0:T(8,128)S(1)} %collective-permute-done.4.raw, f32[264,256]{1,0:T(8,128)S(1)} %convolution_add_fusion.5.refs_0_), custom_call_target="tpu_custom_call" | custom-call | flops 8000000000 | bytes 2000000 | tf_op jit(solution)/shard_map/pallas_call | solution.py:34
  36.1 5.2 %collective-permute-start.5 = (f32[264,256]{1,0:T(8,128)S(1)}, f32[264,256]{1,0:T(8,128)S(1)}, u32[]{:S(2)}, u32[]{:S(2)}) collective-permute-start(f32[264,256]{1,0:T(8,128)S(1)} %get-tuple-element.39), channel_id=1, source_target_pairs={{0,28},{4,24},{8,20},{12,16},{16,12},{20,8},{24,4},{28,0},{1,29},{... | collective-permute-start | bytes 811016 | tf_op jit(solution)/shard_map/ppermute | solution.py:347
  41.3 0.3 fusion.1
  41.6 0.3 fusion.own
  41.9 2.2 %shard_map.78 = (bf16[256,2048]{1,0:T(8,128)(2,1)S(1)}, bf16[256,2048]{1,0:T(8,128)(2,1)S(1)}, f32[8,256]{1,0:T(8,128)S(1)}) custom-call(bf16[256,256]{1,0:T(8,128)(2,1)S(1)} %get-tuple-element.31.top, bf16[256,256]{1,0:T(8,128)(2,1)S(1)} %get-tuple-element.32.rest, f32[264,256]{1,0:T(8,128)S(1)} %fusion.own, f32[16,256]{1,0:T(8,128)S(1)} %copy-done), custom_call_target="tpu_custom_call" | custom-call | flops 1000000000 | bytes 1000000 | tf_op jit(solution)/shard_map/pallas_call | solution.py:34
  44.2 5.6 %collective-permute-done.5 = f32[264,256]{1,0:T(8,128)S(1)} collective-permute-done((f32[264,256]{1,0:T(8,128)S(1)}, f32[264,256]{1,0:T(8,128)S(1)}, u32[]{:S(2)}, u32[]{:S(2)}) %collective-permute-start.5) | collective-permute-done | bytes 270368 | tf_op jit(solution)/shard_map/ppermute | solution.py:347
  49.9 0.3 convolution_add_fusion.2
  50.3 1.5 %collective-permute-done.6 = f32[264,256]{1,0:T(8,128)S(1)} collective-permute-done((f32[264,256]{1,0:T(8,128)S(1)}, f32[264,256]{1,0:T(8,128)S(1)}, u32[]{:S(2)}, u32[]{:S(2)}) %collective-permute-start.6) | collective-permute-done | bytes 270368 | tf_op jit(solution)/shard_map/ppermute | solution.py:365
  51.9 0.1 convolution_add_fusion.8
  52.0 0.7 %collective-permute-start.7 = (f32[1,256]{1,0:T(1,128)S(1)}, f32[1,256]{1,0:T(1,128)S(1)}, u32[]{:S(2)}, u32[]{:S(2)}) collective-permute-start(f32[1,256]{1,0:T(1,128)S(1)} %convolution_add_fusion.8), channel_id=1, source_target_pairs={{0,64},{1,65},{2,66},{3,67},{4,68},{5,69},{6,70},{7,71},{8,72},{9,... | collective-permute-start | bytes 3080 | tf_op jit(solution)/shard_map/ppermute | solution.py:370
  52.7 0.3 convolution_add_fusion
  53.0 1.3 %collective-permute-start.10 = (f32[264,256]{1,0:T(8,128)S(1)}, f32[264,256]{1,0:T(8,128)S(1)}, u32[]{:S(2)}, u32[]{:S(2)}) collective-permute-start(f32[264,256]{1,0:T(8,128)S(1)} %convolution_add_fusion), channel_id=1, source_target_pairs={{128,192},{129,193},{130,194},{131,195},{132,196},{133,197},{134,1... | collective-permute-start | bytes 811016 | tf_op jit(solution)/shard_map/ppermute | solution.py:372
  54.3 0.3 convolution_add_fusion.1.late
  54.6 0.1 convolution_add_fusion.7
  54.7 1.3 %collective-permute-start.9 = (f32[1,256]{1,0:T(1,128)S(1)}, f32[1,256]{1,0:T(1,128)S(1)}, u32[]{:S(2)}, u32[]{:S(2)}) collective-permute-start(f32[1,256]{1,0:T(1,128)S(1)} %convolution_add_fusion.7), channel_id=1, source_target_pairs={{64,192},{65,193},{66,194},{67,195},{68,196},{69,197},{70,198},{71... | collective-permute-start | bytes 3080 | tf_op jit(solution)/shard_map/ppermute | solution.py:377
  56.1 0.7 %collective-permute-start.8 = (f32[1,256]{1,0:T(1,128)S(1)}, f32[1,256]{1,0:T(1,128)S(1)}, u32[]{:S(2)}, u32[]{:S(2)}) collective-permute-start(f32[1,256]{1,0:T(1,128)S(1)} %convolution_add_fusion.7), channel_id=1, source_target_pairs={{64,128},{65,129},{66,130},{67,131},{68,132},{69,133},{70,134},{71... | collective-permute-start | bytes 3080 | tf_op jit(solution)/shard_map/ppermute | solution.py:378
  56.8 5.2 %collective-permute-done.9 = f32[1,256]{1,0:T(1,128)S(1)} collective-permute-done((f32[1,256]{1,0:T(1,128)S(1)}, f32[1,256]{1,0:T(1,128)S(1)}, u32[]{:S(2)}, u32[]{:S(2)}) %collective-permute-start.9) | collective-permute-done | bytes 1056 | tf_op jit(solution)/shard_map/ppermute | solution.py:377
  61.9 1.5 %collective-permute-done.10 = f32[264,256]{1,0:T(8,128)S(1)} collective-permute-done((f32[264,256]{1,0:T(8,128)S(1)}, f32[264,256]{1,0:T(8,128)S(1)}, u32[]{:S(2)}, u32[]{:S(2)}) %collective-permute-start.10) | collective-permute-done | bytes 270368 | tf_op jit(solution)/shard_map/ppermute | solution.py:372
  63.6 1.3 %shard_map.79 = f32[8,256]{1,0:T(8,128)} custom-call(f32[1,256]{1,0:T(1,128)S(1)} %broadcast_select_fusion.10.entry, f32[264,256]{1,0:T(8,128)S(1)} %convolution_add_fusion.1.late, bf16[256,2048]{1,0:T(8,128)(2,1)S(1)} %get-tuple-element.52.maps_top, bf16[256,2048]{1,0:T(8,128)(2,1)S(1)} %get-tuple-element.53.maps_rest, f32[8,256]{1,0:T(8,128)S(1)} %get-tuple-element.54.states), custom_call_target="tpu_custom_call" | custom-call | flops 100000000 | bytes 1000000 | tf_op jit(solution)/shard_map/pallas_call | solution.py:34
  (26 shorter events, 0.5 us)
Async XLA Ops:
  0.0 9.4 %copy-start.1 = (f32[256,256]{1,0:T(8,128)S(1)}, f32[256,256]{1,0:T(8,128)}, u32[]{:S(2)}) copy-start(f32[256,256]{1,0:T(8,128)} %source) | copy-start | bytes 786436
  4.5 4.8 %copy-start = (f32[16,256]{1,0:T(8,128)S(1)}, f32[16,256]{1,0:T(8,128)}, u32[]{:S(2)}) copy-start(f32[16,256]{1,0:T(8,128)} %shard_map.73.raw) | copy-start | bytes 49156
  4.5 6.0 %collective-permute-start = (f32[16,256]{1,0:T(8,128)}, f32[16,256]{1,0:T(8,128)S(1)}, u32[]{:S(2)}, u32[]{:S(2)}) collective-permute-start(f32[16,256]{1,0:T(8,128)} %shard_map.73.raw), channel_id=1, source_target_pairs={{0,1},{1,0},{2,3},{3,2},{4,5},{5,4},{6,7},{7,6},{8,9},{9,8},{10,11... | collective-permute-start | bytes 49160 | tf_op jit(solution)/shard_map/ppermute | solution.py:332
  6.2 5.5 %collective-permute-start.1 = (f32[16,256]{1,0:T(8,128)}, f32[16,256]{1,0:T(8,128)S(1)}, u32[]{:S(2)}, u32[]{:S(2)}) collective-permute-start(f32[16,256]{1,0:T(8,128)} %shard_map.73.raw), channel_id=1, source_target_pairs={{0,2},{1,3},{2,0},{3,1},{4,6},{5,7},{6,4},{7,5},{8,10},{9,11},{10,... | collective-permute-start | bytes 49160 | tf_op jit(solution)/shard_map/ppermute | solution.py:332
  9.1 5.2 %collective-permute-start.2 = (f32[16,256]{1,0:T(8,128)}, f32[16,256]{1,0:T(8,128)S(1)}, u32[]{:S(2)}, u32[]{:S(2)}) collective-permute-start(f32[16,256]{1,0:T(8,128)} %shard_map.73.raw), channel_id=1, source_target_pairs={{0,3},{1,2},{2,1},{3,0},{4,7},{5,6},{6,5},{7,4},{8,11},{9,10},{10,... | collective-permute-start | bytes 49160 | tf_op jit(solution)/shard_map/ppermute | solution.py:332
  14.3 5.7 %collective-permute-start.3 = (f32[64,256]{1,0:T(8,128)S(1)}, f32[64,256]{1,0:T(8,128)S(1)}, u32[]{:S(2)}, u32[]{:S(2)}) collective-permute-start(f32[64,256]{1,0:T(8,128)S(1)} %get-tuple-element.59.raw), channel_id=1, source_target_pairs={{0,4},{4,0},{8,12},{12,8},{16,20},{20,16},{24,28},{28,24},{1,5},{5... | collective-permute-start | bytes 196616 | tf_op jit(solution)/shard_map/ppermute | solution.py:334
  20.0 7.6 %collective-permute-start.4 = (f32[128,256]{1,0:T(8,128)S(1)}, f32[128,256]{1,0:T(8,128)S(1)}, u32[]{:S(2)}, u32[]{:S(2)}) collective-permute-start(f32[128,256]{1,0:T(8,128)S(1)} %constant_dynamic-update-slice_fusion.4), channel_id=1, source_target_pairs={{0,8},{4,12},{8,0},{12,4},{16,24},{20,28},{24,16},{28,20},{1,9},{5... | collective-permute-start | bytes 393224 | tf_op jit(solution)/shard_map/ppermute | solution.py:337
  36.1 13.7 %collective-permute-start.5 = (f32[264,256]{1,0:T(8,128)S(1)}, f32[264,256]{1,0:T(8,128)S(1)}, u32[]{:S(2)}, u32[]{:S(2)}) collective-permute-start(f32[264,256]{1,0:T(8,128)S(1)} %get-tuple-element.39), channel_id=1, source_target_pairs={{0,28},{4,24},{8,20},{12,16},{16,12},{20,8},{24,4},{28,0},{1,29},{... | collective-permute-start | bytes 811016 | tf_op jit(solution)/shard_map/ppermute | solution.py:347
  50.2 1.6 %collective-permute-start.6 = (f32[264,256]{1,0:T(8,128)S(1)}, f32[264,256]{1,0:T(8,128)S(1)}, u32[]{:S(2)}, u32[]{:S(2)}) collective-permute-start(f32[264,256]{1,0:T(8,128)S(1)} %convolution_add_fusion.2), channel_id=1, source_target_pairs={{0,32},{32,0},{1,33},{33,1},{2,34},{34,2},{3,35},{35,3},{4,36},{36... | collective-permute-start | bytes 811016 | tf_op jit(solution)/shard_map/ppermute | solution.py:365
  52.0 2.6 %collective-permute-start.7 = (f32[1,256]{1,0:T(1,128)S(1)}, f32[1,256]{1,0:T(1,128)S(1)}, u32[]{:S(2)}, u32[]{:S(2)}) collective-permute-start(f32[1,256]{1,0:T(1,128)S(1)} %convolution_add_fusion.8), channel_id=1, source_target_pairs={{0,64},{1,65},{2,66},{3,67},{4,68},{5,69},{6,70},{7,71},{8,72},{9,... | collective-permute-start | bytes 3080 | tf_op jit(solution)/shard_map/ppermute | solution.py:370
  53.0 10.4 %collective-permute-start.10 = (f32[264,256]{1,0:T(8,128)S(1)}, f32[264,256]{1,0:T(8,128)S(1)}, u32[]{:S(2)}, u32[]{:S(2)}) collective-permute-start(f32[264,256]{1,0:T(8,128)S(1)} %convolution_add_fusion), channel_id=1, source_target_pairs={{128,192},{129,193},{130,194},{131,195},{132,196},{133,197},{134,1... | collective-permute-start | bytes 811016 | tf_op jit(solution)/shard_map/ppermute | solution.py:372
  54.7 7.2 %collective-permute-start.9 = (f32[1,256]{1,0:T(1,128)S(1)}, f32[1,256]{1,0:T(1,128)S(1)}, u32[]{:S(2)}, u32[]{:S(2)}) collective-permute-start(f32[1,256]{1,0:T(1,128)S(1)} %convolution_add_fusion.7), channel_id=1, source_target_pairs={{64,192},{65,193},{66,194},{67,195},{68,196},{69,197},{70,198},{71... | collective-permute-start | bytes 3080 | tf_op jit(solution)/shard_map/ppermute | solution.py:377
  56.1 7.5 %collective-permute-start.8 = (f32[1,256]{1,0:T(1,128)S(1)}, f32[1,256]{1,0:T(1,128)S(1)}, u32[]{:S(2)}, u32[]{:S(2)}) collective-permute-start(f32[1,256]{1,0:T(1,128)S(1)} %convolution_add_fusion.7), channel_id=1, source_target_pairs={{64,128},{65,129},{66,130},{67,131},{68,132},{69,133},{70,134},{71... | collective-permute-start | bytes 3080 | tf_op jit(solution)/shard_map/ppermute | solution.py:378

commit v4 on v3

--- a/solution.py
+++ b/solution.py
@@ -211,8 +211,7 @@
 def maps_kernel(mine, top, rest, raw, *refs):
     refs, place = refs[:-1], refs[-1]
     groups, count, rows, width = place.shape
-    known = refs[0] if groups == 2 else None
-    refs = refs[1:] if groups == 2 else refs
+    known, refs = (refs[:0], refs) if mine else (refs[: 3 - groups], refs[3 - groups :])
     local, spare = rows // 2, 16
     me = lax.axis_index("y")
     for group in range(groups):
@@ -258,7 +257,7 @@
         results.append(before)
         if mine:
             refs[1][...] = prefix[: width + 8]
-    if groups == 1:
+    if mine:
         refs[0][...] = results[0][: width + 8]
         return
 
@@ -268,15 +267,21 @@
 
     z = lax.axis_index("z")
     odd, second = lax.rem(z, 2) == 1, lax.rem(z, 4) >= 2
+    known = [jnp.concatenate([ref[...], ref[width:, :]], 0) for ref in known]
+    if groups == 1:
+        group, before = known
+        other = results[0]
+        refs[0][...] = joined(jnp.where(odd, other, group), jnp.where(odd, group, other))[: width + 8]
+        refs[1][...] = jnp.where(odd, joined(other, before), before)[: width + 8]
+        return
     pair = joined(*(jnp.where(odd, results[1 - k], results[k]) for k in range(2)))
-    known = jnp.concatenate([known[...], known[width:, :]], 0)
-    refs[0][...] = joined(jnp.where(second, pair, known), jnp.where(second, known, pair))[: width + 8]
+    refs[0][...] = joined(jnp.where(second, pair, known[0]), jnp.where(second, known[0], pair))[: width + 8]
     refs[1][...] = pair[: width + 8]
 
 
 def group_maps(mine, top, rest, raw, *known):
     width, groups = raw.shape[1], raw.shape[0] // 64
-    outs = [((width + 8, width), F32)] * (2 if mine or known else 1)
+    outs = [((width + 8, width), F32)] * 2
     scratch = [((groups, 4, 16, width), F32)]
     cost = 4 * 10**9 * groups
     return call(functools.partial(maps_kernel, mine), outs, scratch, cost, 2 * 10**6, top, rest, raw, *known)
@@ -335,16 +340,12 @@
     group, own = group_maps(True, top, rest, rows)
     beside, group = lax.optimization_barrier((beside, group))
     across = lax.ppermute(jnp.concatenate([rows, beside], 0), "z", exchange_pairs(2, count_z))
-    (other,) = group_maps(False, top, rest, beside)
-    across, other = lax.optimization_barrier((across, other))
-
-    odd, second = (me_z & 1) > 0, (me_z & 2) > 0
-    low, high = jnp.where(odd, other, group), jnp.where(odd, group, other)
-    pair = join(low, high)
+    pair, own = group_maps(False, top, rest, beside, group, own)
+    across, pair = lax.optimization_barrier((across, pair))
     block, other_pair = group_maps(False, top, rest, across, pair)
-    own = jnp.where(odd, join(low, own), own)
-
-    other = lax.ppermute(block, "z", exchange_pairs(4, count_z))
+    second = (me_z & 2) > 0
+
+    other = lax.ppermute(block, "z", [(i, i ^ 6) for i in range(count_z)])
     own = jnp.where(second, join(other_pair, own), own)
     ahead = call(
         ahead_kernel,

time: 65 us -> 64.9 us (level)
  starting transfers between devices: 19.5 us -> 18.5 us
    ppermute x1, starting transfers between devices: 5.21 us -> 4.19 us  [on_device(): other = lax.ppermute(block, 'z', [(i, i ^ 6) for i in range(count_z)])]
    ppermute x1, waiting for transfers between devices: 5.64 us -> 6.44 us  [on_device(): other = lax.ppermute(block, 'z', [(i, i ^ 6) for i in range(count_z)])]
    dot_general x9 -> x7, matrix products: 2.14 us -> 1.56 us  [dot(): jnp.dot(a, b, precision=lax.Precision.HIGH, preferred_element_type=F32)]
  transfers between devices with their start and end apart: 11 -> 11, of which waited for: 7 -> 6; matrix products, arithmetic and copies ran while one was open for 2% -> 2% of each run, Pallas kernels for 17% -> 18%
where the time goes in v4:
time: 64.9 us; the launch traced here: 64.2 us
  Pallas kernels  25.3 us (39%)
  starting transfers between devices  18.5 us (29%)
  waiting for transfers between devices  18.3 us (28%)
  matrix products  1.56 us (2%)
    pallas_call x6, Pallas kernels, call(): pl.pallas_call(kernel, out_shape=[jax.ShapeDtypeStruct(shape, kind) for s...  20.8 us
    ppermute x1, waiting for transfers between devices, on_device(): other = lax.ppermute(block, 'z', [(i, i ^ 6) for i in range(count_z)])  6.44 us
    ppermute x1, waiting for transfers between devices, on_device(): for_fourth = lax.ppermute(leaving, 'x', [(1, 3)])  5.15 us
    ppermute x3, starting transfers between devices, on_device(): lax.ppermute(raw, 'y', [(i, i ^ k) for i in range(count_y)])  4.79 us
    pallas_call x1, Pallas kernels, encode(): pl.pallas_call(encoder_kernel, out_shape=jax.ShapeDtypeStruct((2 * local,...  4.51 us
    ppermute x1, starting transfers between devices, on_device(): other = lax.ppermute(block, 'z', [(i, i ^ 6) for i in range(count_z)])  4.19 us
    ppermute x3, waiting for transfers between devices, on_device(): lax.ppermute(raw, 'y', [(i, i ^ k) for i in range(count_y)])  3.68 us
    ppermute x1, starting transfers between devices, on_device(): lax.ppermute(jnp.concatenate([rows, beside], 0), 'z', exchange_pairs(2, c...  3.54 us
  transfers between devices with their start and end apart: 11, of which 6 were waited for; matrix products, arithmetic and copies ran while one was open for 2% of the time, Pallas kernels for 18%

profile of v4, /device:TPU:6, one launch (start us, length us, event | category | flops | bytes accessed | tf_op | source)
XLA Modules:
  0.0 64.2 jit_solution(15871290560800033009)
XLA Ops:
  0.0 4.5 %shard_map.73.raw = f32[16,256]{1,0:T(8,128)} custom-call(bf16[8,64,192]{2,1,0:T(8,128)(2,1)} %refs_0_.1, bf16[4,3,4,64]{3,2,1,0:T(4,128)(2,1)} %bitcast.22, bf16[4,256,128]{2,1,0:T(8,128)(2,1)} %bitcast.21, bf16[4,512,256]{2,1,0:T(8,128)(2,1)} %bitcast.20, bf16[256,256]{1,0:T(8,128)(2,1)} %refs_4_.1, f32[8,256]{1,0:T(8,128)} %refs_5_.1), custom_call_target="tpu_custom_call" | custom-call | flops 5000000000 | bytes 2000000 | tf_op jit(solution)/shard_map/pallas_call | solution.py:198
  4.5 1.7 %collective-permute-start = (f32[16,256]{1,0:T(8,128)}, f32[16,256]{1,0:T(8,128)S(1)}, u32[]{:S(2)}, u32[]{:S(2)}) collective-permute-start(f32[16,256]{1,0:T(8,128)} %shard_map.73.raw), channel_id=1, source_target_pairs={{0,1},{1,0},{2,3},{3,2},{4,5},{5,4},{6,7},{7,6},{8,9},{9,8},{10,11... | collective-permute-start | bytes 49160 | tf_op jit(solution)/shard_map/ppermute | solution.py:337
  6.2 2.9 %collective-permute-start.1 = (f32[16,256]{1,0:T(8,128)}, f32[16,256]{1,0:T(8,128)S(1)}, u32[]{:S(2)}, u32[]{:S(2)}) collective-permute-start(f32[16,256]{1,0:T(8,128)} %shard_map.73.raw), channel_id=1, source_target_pairs={{0,2},{1,3},{2,0},{3,1},{4,6},{5,7},{6,4},{7,5},{8,10},{9,11},{10,... | collective-permute-start | bytes 49160 | tf_op jit(solution)/shard_map/ppermute | solution.py:337
  9.1 0.2 collective-permute-start.2
  9.4 1.2 %shard_map.74 = (bf16[256,256]{1,0:T(8,128)(2,1)S(1)}, bf16[256,256]{1,0:T(8,128)(2,1)S(1)}) custom-call(f32[256,256]{1,0:T(8,128)S(1)} %copy-done.1), custom_call_target="tpu_custom_call" | custom-call | flops 1000000000 | bytes 1000000 | tf_op jit(solution)/shard_map/pallas_call | solution.py:34
  10.6 1.1 %collective-permute-done.1 = f32[16,256]{1,0:T(8,128)S(1)} collective-permute-done((f32[16,256]{1,0:T(8,128)}, f32[16,256]{1,0:T(8,128)S(1)}, u32[]{:S(2)}, u32[]{:S(2)}) %collective-permute-start.1) | collective-permute-done | bytes 16416 | tf_op jit(solution)/shard_map/ppermute | solution.py:337
  11.7 2.6 %collective-permute-done.2 = f32[16,256]{1,0:T(8,128)S(1)} collective-permute-done((f32[16,256]{1,0:T(8,128)}, f32[16,256]{1,0:T(8,128)S(1)}, u32[]{:S(2)}, u32[]{:S(2)}) %collective-permute-start.2) | collective-permute-done | bytes 16416 | tf_op jit(solution)/shard_map/ppermute | solution.py:337
  14.3 1.9 %collective-permute-start.3 = (f32[64,256]{1,0:T(8,128)S(1)}, f32[64,256]{1,0:T(8,128)S(1)}, u32[]{:S(2)}, u32[]{:S(2)}) collective-permute-start(f32[64,256]{1,0:T(8,128)S(1)} %get-tuple-element.63.raw), channel_id=1, source_target_pairs={{0,4},{4,0},{8,12},{12,8},{16,20},{20,16},{24,28},{28,24},{1,5},{5... | collective-permute-start | bytes 196616 | tf_op jit(solution)/shard_map/ppermute | solution.py:339
  16.2 3.8 %shard_map.75 = (f32[264,256]{1,0:T(8,128)S(1)}, f32[264,256]{1,0:T(8,128)S(1)}) custom-call(bf16[256,256]{1,0:T(8,128)(2,1)S(1)} %get-tuple-element.33.top, bf16[256,256]{1,0:T(8,128)(2,1)S(1)} %get-tuple-element.34.rest, f32[64,256]{1,0:T(8,128)S(1)} %get-tuple-element.63.raw), custom_call_target="tpu_custom_call" | custom-call | flops 4000000000 | bytes 2000000 | tf_op jit(solution)/shard_map/pallas_call | solution.py:34
  20.0 3.5 %collective-permute-start.4 = (f32[128,256]{1,0:T(8,128)S(1)}, f32[128,256]{1,0:T(8,128)S(1)}, u32[]{:S(2)}, u32[]{:S(2)}) collective-permute-start(f32[128,256]{1,0:T(8,128)S(1)} %constant_dynamic-update-slice_fusion.4), channel_id=1, source_target_pairs={{0,8},{4,12},{8,0},{12,4},{16,24},{20,28},{24,16},{28,20},{1,9},{5... | collective-permute-start | bytes 393224 | tf_op jit(solution)/shard_map/ppermute | solution.py:342
  23.6 4.2 %shard_map.76 = (f32[264,256]{1,0:T(8,128)S(1)}, f32[264,256]{1,0:T(8,128)S(1)}) custom-call(bf16[256,256]{1,0:T(8,128)(2,1)S(1)} %get-tuple-element.33.top, bf16[256,256]{1,0:T(8,128)(2,1)S(1)} %get-tuple-element.34.rest, f32[64,256]{1,0:T(8,128)S(1)} %collective-permute-done.3.raw, f32[264,256]{1,0:T(8,128)S(1)} %get-tuple-element.38.refs_0_, ...), custom_call_target="tpu_custom_call" | custom-call | flops 4000000000 | bytes 2000000 | tf_op jit(solution)/shard_map/pallas_call | solution.py:34
  27.8 8.2 %shard_map.77 = (f32[264,256]{1,0:T(8,128)S(1)}, f32[264,256]{1,0:T(8,128)S(1)}) custom-call(bf16[256,256]{1,0:T(8,128)(2,1)S(1)} %get-tuple-element.33.top, bf16[256,256]{1,0:T(8,128)(2,1)S(1)} %get-tuple-element.34.rest, f32[128,256]{1,0:T(8,128)S(1)} %collective-permute-done.4.raw, f32[264,256]{1,0:T(8,128)S(1)} %get-tuple-element.42.refs_0_), custom_call_target="tpu_custom_call" | custom-call | flops 8000000000 | bytes 2000000 | tf_op jit(solution)/shard_map/pallas_call | solution.py:34
  36.0 4.2 %collective-permute-start.5 = (f32[264,256]{1,0:T(8,128)S(1)}, f32[264,256]{1,0:T(8,128)S(1)}, u32[]{:S(2)}, u32[]{:S(2)}) collective-permute-start(f32[264,256]{1,0:T(8,128)S(1)} %get-tuple-element.43), channel_id=1, source_target_pairs={{0,24},{4,28},{8,16},{12,20},{16,8},{20,12},{24,0},{28,4},{1,25},{... | collective-permute-start | bytes 811016 | tf_op jit(solution)/shard_map/ppermute | solution.py:348
  40.1 0.3 fusion.own
  40.4 2.2 %shard_map.78 = (bf16[256,2048]{1,0:T(8,128)(2,1)S(1)}, bf16[256,2048]{1,0:T(8,128)(2,1)S(1)}, f32[8,256]{1,0:T(8,128)S(1)}) custom-call(bf16[256,256]{1,0:T(8,128)(2,1)S(1)} %get-tuple-element.33.top, bf16[256,256]{1,0:T(8,128)(2,1)S(1)} %get-tuple-element.34.rest, f32[264,256]{1,0:T(8,128)S(1)} %fusion.own, f32[16,256]{1,0:T(8,128)S(1)} %copy-done), custom_call_target="tpu_custom_call" | custom-call | flops 1000000000 | bytes 1000000 | tf_op jit(solution)/shard_map/pallas_call | solution.py:34
  42.7 6.4 %collective-permute-done.5 = f32[264,256]{1,0:T(8,128)S(1)} collective-permute-done((f32[264,256]{1,0:T(8,128)S(1)}, f32[264,256]{1,0:T(8,128)S(1)}, u32[]{:S(2)}, u32[]{:S(2)}) %collective-permute-start.5) | collective-permute-done | bytes 270368 | tf_op jit(solution)/shard_map/ppermute | solution.py:348
  49.2 0.3 convolution_add_fusion.2
  49.4 0.1 collective-permute-start.6
  49.6 1.5 %collective-permute-done.6 = f32[264,256]{1,0:T(8,128)S(1)} collective-permute-done((f32[264,256]{1,0:T(8,128)S(1)}, f32[264,256]{1,0:T(8,128)S(1)}, u32[]{:S(2)}, u32[]{:S(2)}) %collective-permute-start.6) | collective-permute-done | bytes 270368 | tf_op jit(solution)/shard_map/ppermute | solution.py:366
  51.1 0.1 convolution_add_fusion.6
  51.3 0.7 %collective-permute-start.7 = (f32[1,256]{1,0:T(1,128)S(1)}, f32[1,256]{1,0:T(1,128)S(1)}, u32[]{:S(2)}, u32[]{:S(2)}) collective-permute-start(f32[1,256]{1,0:T(1,128)S(1)} %convolution_add_fusion.6), channel_id=1, source_target_pairs={{0,64},{1,65},{2,66},{3,67},{4,68},{5,69},{6,70},{7,71},{8,72},{9,... | collective-permute-start | bytes 3080 | tf_op jit(solution)/shard_map/ppermute | solution.py:371
  52.0 0.3 convolution_add_fusion
  52.3 1.3 %collective-permute-start.10 = (f32[264,256]{1,0:T(8,128)S(1)}, f32[264,256]{1,0:T(8,128)S(1)}, u32[]{:S(2)}, u32[]{:S(2)}) collective-permute-start(f32[264,256]{1,0:T(8,128)S(1)} %convolution_add_fusion), channel_id=1, source_target_pairs={{128,192},{129,193},{130,194},{131,195},{132,196},{133,197},{134,1... | collective-permute-start | bytes 811016 | tf_op jit(solution)/shard_map/ppermute | solution.py:373
  53.6 0.3 convolution_add_fusion.1.late
  53.9 0.1 convolution_add_fusion.5
  54.0 1.3 %collective-permute-start.9 = (f32[1,256]{1,0:T(1,128)S(1)}, f32[1,256]{1,0:T(1,128)S(1)}, u32[]{:S(2)}, u32[]{:S(2)}) collective-permute-start(f32[1,256]{1,0:T(1,128)S(1)} %convolution_add_fusion.5), channel_id=1, source_target_pairs={{64,192},{65,193},{66,194},{67,195},{68,196},{69,197},{70,198},{71... | collective-permute-start | bytes 3080 | tf_op jit(solution)/shard_map/ppermute | solution.py:378
  55.4 0.7 %collective-permute-start.8 = (f32[1,256]{1,0:T(1,128)S(1)}, f32[1,256]{1,0:T(1,128)S(1)}, u32[]{:S(2)}, u32[]{:S(2)}) collective-permute-start(f32[1,256]{1,0:T(1,128)S(1)} %convolution_add_fusion.5), channel_id=1, source_target_pairs={{64,128},{65,129},{66,130},{67,131},{68,132},{69,133},{70,134},{71... | collective-permute-start | bytes 3080 | tf_op jit(solution)/shard_map/ppermute | solution.py:379
  56.0 5.1 %collective-permute-done.9 = f32[1,256]{1,0:T(1,128)S(1)} collective-permute-done((f32[1,256]{1,0:T(1,128)S(1)}, f32[1,256]{1,0:T(1,128)S(1)}, u32[]{:S(2)}, u32[]{:S(2)}) %collective-permute-start.9) | collective-permute-done | bytes 1056 | tf_op jit(solution)/shard_map/ppermute | solution.py:378
  61.2 1.5 %collective-permute-done.10 = f32[264,256]{1,0:T(8,128)S(1)} collective-permute-done((f32[264,256]{1,0:T(8,128)S(1)}, f32[264,256]{1,0:T(8,128)S(1)}, u32[]{:S(2)}, u32[]{:S(2)}) %collective-permute-start.10) | collective-permute-done | bytes 270368 | tf_op jit(solution)/shard_map/ppermute | solution.py:373
  62.7 0.1 convolution_add_fusion.4
  62.8 0.1 broadcast_select_fusion.6.entry
  62.9 1.3 %shard_map.79 = f32[8,256]{1,0:T(8,128)} custom-call(f32[1,256]{1,0:T(1,128)S(1)} %broadcast_select_fusion.6.entry, f32[264,256]{1,0:T(8,128)S(1)} %convolution_add_fusion.1.late, bf16[256,2048]{1,0:T(8,128)(2,1)S(1)} %get-tuple-element.56.maps_top, bf16[256,2048]{1,0:T(8,128)(2,1)S(1)} %get-tuple-element.57.maps_rest, f32[8,256]{1,0:T(8,128)S(1)} %get-tuple-element.58.states), custom_call_target="tpu_custom_call" | custom-call | flops 100000000 | bytes 1000000 | tf_op jit(solution)/shard_map/pallas_call | solution.py:34
  (21 shorter events, 0.2 us)
Async XLA Ops:
  0.0 9.4 %copy-start.1 = (f32[256,256]{1,0:T(8,128)S(1)}, f32[256,256]{1,0:T(8,128)}, u32[]{:S(2)}) copy-start(f32[256,256]{1,0:T(8,128)} %source) | copy-start | bytes 786436
  4.5 4.8 %copy-start = (f32[16,256]{1,0:T(8,128)S(1)}, f32[16,256]{1,0:T(8,128)}, u32[]{:S(2)}) copy-start(f32[16,256]{1,0:T(8,128)} %shard_map.73.raw) | copy-start | bytes 49156
  4.5 6.0 %collective-permute-start = (f32[16,256]{1,0:T(8,128)}, f32[16,256]{1,0:T(8,128)S(1)}, u32[]{:S(2)}, u32[]{:S(2)}) collective-permute-start(f32[16,256]{1,0:T(8,128)} %shard_map.73.raw), channel_id=1, source_target_pairs={{0,1},{1,0},{2,3},{3,2},{4,5},{5,4},{6,7},{7,6},{8,9},{9,8},{10,11... | collective-permute-start | bytes 49160 | tf_op jit(solution)/shard_map/ppermute | solution.py:337
  6.2 5.5 %collective-permute-start.1 = (f32[16,256]{1,0:T(8,128)}, f32[16,256]{1,0:T(8,128)S(1)}, u32[]{:S(2)}, u32[]{:S(2)}) collective-permute-start(f32[16,256]{1,0:T(8,128)} %shard_map.73.raw), channel_id=1, source_target_pairs={{0,2},{1,3},{2,0},{3,1},{4,6},{5,7},{6,4},{7,5},{8,10},{9,11},{10,... | collective-permute-start | bytes 49160 | tf_op jit(solution)/shard_map/ppermute | solution.py:337
  9.1 5.2 %collective-permute-start.2 = (f32[16,256]{1,0:T(8,128)}, f32[16,256]{1,0:T(8,128)S(1)}, u32[]{:S(2)}, u32[]{:S(2)}) collective-permute-start(f32[16,256]{1,0:T(8,128)} %shard_map.73.raw), channel_id=1, source_target_pairs={{0,3},{1,2},{2,1},{3,0},{4,7},{5,6},{6,5},{7,4},{8,11},{9,10},{10,... | collective-permute-start | bytes 49160 | tf_op jit(solution)/shard_map/ppermute | solution.py:337
  14.3 5.7 %collective-permute-start.3 = (f32[64,256]{1,0:T(8,128)S(1)}, f32[64,256]{1,0:T(8,128)S(1)}, u32[]{:S(2)}, u32[]{:S(2)}) collective-permute-start(f32[64,256]{1,0:T(8,128)S(1)} %get-tuple-element.63.raw), channel_id=1, source_target_pairs={{0,4},{4,0},{8,12},{12,8},{16,20},{20,16},{24,28},{28,24},{1,5},{5... | collective-permute-start | bytes 196616 | tf_op jit(solution)/shard_map/ppermute | solution.py:339
  20.0 7.7 %collective-permute-start.4 = (f32[128,256]{1,0:T(8,128)S(1)}, f32[128,256]{1,0:T(8,128)S(1)}, u32[]{:S(2)}, u32[]{:S(2)}) collective-permute-start(f32[128,256]{1,0:T(8,128)S(1)} %constant_dynamic-update-slice_fusion.4), channel_id=1, source_target_pairs={{0,8},{4,12},{8,0},{12,4},{16,24},{20,28},{24,16},{28,20},{1,9},{5... | collective-permute-start | bytes 393224 | tf_op jit(solution)/shard_map/ppermute | solution.py:342
  36.0 13.2 %collective-permute-start.5 = (f32[264,256]{1,0:T(8,128)S(1)}, f32[264,256]{1,0:T(8,128)S(1)}, u32[]{:S(2)}, u32[]{:S(2)}) collective-permute-start(f32[264,256]{1,0:T(8,128)S(1)} %get-tuple-element.43), channel_id=1, source_target_pairs={{0,24},{4,28},{8,16},{12,20},{16,8},{20,12},{24,0},{28,4},{1,25},{... | collective-permute-start | bytes 811016 | tf_op jit(solution)/shard_map/ppermute | solution.py:348
  49.4 1.6 %collective-permute-start.6 = (f32[264,256]{1,0:T(8,128)S(1)}, f32[264,256]{1,0:T(8,128)S(1)}, u32[]{:S(2)}, u32[]{:S(2)}) collective-permute-start(f32[264,256]{1,0:T(8,128)S(1)} %convolution_add_fusion.2), channel_id=1, source_target_pairs={{0,32},{32,0},{1,33},{33,1},{2,34},{34,2},{3,35},{35,3},{4,36},{36... | collective-permute-start | bytes 811016 | tf_op jit(solution)/shard_map/ppermute | solution.py:366
  51.3 2.6 %collective-permute-start.7 = (f32[1,256]{1,0:T(1,128)S(1)}, f32[1,256]{1,0:T(1,128)S(1)}, u32[]{:S(2)}, u32[]{:S(2)}) collective-permute-start(f32[1,256]{1,0:T(1,128)S(1)} %convolution_add_fusion.6), channel_id=1, source_target_pairs={{0,64},{1,65},{2,66},{3,67},{4,68},{5,69},{6,70},{7,71},{8,72},{9,... | collective-permute-start | bytes 3080 | tf_op jit(solution)/shard_map/ppermute | solution.py:371
  52.3 10.4 %collective-permute-start.10 = (f32[264,256]{1,0:T(8,128)S(1)}, f32[264,256]{1,0:T(8,128)S(1)}, u32[]{:S(2)}, u32[]{:S(2)}) collective-permute-start(f32[264,256]{1,0:T(8,128)S(1)} %convolution_add_fusion), channel_id=1, source_target_pairs={{128,192},{129,193},{130,194},{131,195},{132,196},{133,197},{134,1... | collective-permute-start | bytes 811016 | tf_op jit(solution)/shard_map/ppermute | solution.py:373
  54.0 7.2 %collective-permute-start.9 = (f32[1,256]{1,0:T(1,128)S(1)}, f32[1,256]{1,0:T(1,128)S(1)}, u32[]{:S(2)}, u32[]{:S(2)}) collective-permute-start(f32[1,256]{1,0:T(1,128)S(1)} %convolution_add_fusion.5), channel_id=1, source_target_pairs={{64,192},{65,193},{66,194},{67,195},{68,196},{69,197},{70,198},{71... | collective-permute-start | bytes 3080 | tf_op jit(solution)/shard_map/ppermute | solution.py:378
  55.4 7.5 %collective-permute-start.8 = (f32[1,256]{1,0:T(1,128)S(1)}, f32[1,256]{1,0:T(1,128)S(1)}, u32[]{:S(2)}, u32[]{:S(2)}) collective-permute-start(f32[1,256]{1,0:T(1,128)S(1)} %convolution_add_fusion.5), channel_id=1, source_target_pairs={{64,128},{65,129},{66,130},{67,131},{68,132},{69,133},{70,134},{71... | collective-permute-start | bytes 3080 | tf_op jit(solution)/shard_map/ppermute | solution.py:379

commit v5 on v4

--- a/solution.py
+++ b/solution.py
@@ -365,12 +365,11 @@
 
     other = lax.ppermute(block, "core", exchange_pairs(1, 2))
     low_core, high_core = jnp.where(me_core > 0, other, block), jnp.where(me_core > 0, block, other)
-    block_end = dot(low_core[width : width + 1], high_core[:width]) + high_core[width : width + 1]
-    block_end, low_core = lax.optimization_barrier((block_end, low_core))
-
-    first_end = lax.ppermute(block_end, "x", [(0, 1)])
+
     block = join(low_core, high_core)
     third = lax.ppermute(block, "x", [(2, 3)])
+    block_end = block[width : width + 1]
+    first_end = lax.ppermute(block_end, "x", [(0, 1)])
     still = jnp.concatenate([jnp.eye(width, dtype=F32), jnp.zeros((8, width), F32)], 0)
     late = join(jnp.where(me_core > 0, low_core, still), jnp.where(upper, low_half, still))
     first_end, late = lax.optimization_barrier((first_end, late))

time: 64.9 us -> 66 us (1.017)
  local copies, waits for them, and re-layouts: 0.04 us -> 1.22 us
  waiting for transfers between devices: 18.3 us -> 17.3 us
  matrix products: 1.56 us -> 2.37 us
    ppermute x1, waiting for transfers between devices: 5.15 us -> 6.78 us  [on_device(): for_fourth = lax.ppermute(leaving, 'x', [(1, 3)])]
    ppermute x1, waiting for transfers between devices: 1.5 us -> 0.01 us  [on_device(): third = lax.ppermute(block, 'x', [(2, 3)])]
    unnamed x7, local copies, waits for them, and re-layouts: 0.02 us -> 1.19 us
    dot_general x7 -> x6, matrix products: 1.56 us -> 2.37 us  [dot(): jnp.dot(a, b, precision=lax.Precision.HIGH, preferred_element_type=F32)]
    ppermute x3, waiting for transfers between devices: 3.68 us -> 2.95 us  [on_device(): lax.ppermute(raw, 'y', [(i, i ^ k) for i in range(count_y)])]
  transfers between devices with their start and end apart: 11 -> 11, of which waited for: 6 -> 5; matrix products, arithmetic and copies ran while one was open for 2% -> 4% of each run, Pallas kernels for 18% -> 17%
where the time goes in v5:
time: 66 us; the launch traced here: 65.1 us
  Pallas kernels  25.3 us (38%)
  starting transfers between devices  18.5 us (28%)
  waiting for transfers between devices  17.3 us (26%)
  matrix products  2.37 us (4%)
  local copies, waits for them, and re-layouts  1.22 us (2%)
    pallas_call x6, Pallas kernels, call(): pl.pallas_call(kernel, out_shape=[jax.ShapeDtypeStruct(shape, kind) for s...  20.8 us
    ppermute x1, waiting for transfers between devices, on_device(): for_fourth = lax.ppermute(leaving, 'x', [(1, 3)])  6.78 us
    ppermute x1, waiting for transfers between devices, on_device(): other = lax.ppermute(block, 'z', [(i, i ^ 6) for i in range(count_z)])  6.02 us
    ppermute x3, starting transfers between devices, on_device(): lax.ppermute(raw, 'y', [(i, i ^ k) for i in range(count_y)])  4.79 us
    pallas_call x1, Pallas kernels, encode(): pl.pallas_call(encoder_kernel, out_shape=jax.ShapeDtypeStruct((2 * local,...  4.5 us
    ppermute x1, starting transfers between devices, on_device(): other = lax.ppermute(block, 'z', [(i, i ^ 6) for i in range(count_z)])  4.19 us
    ppermute x1, starting transfers between devices, on_device(): lax.ppermute(jnp.concatenate([rows, beside], 0), 'z', exchange_pairs(2, c...  3.54 us
    ppermute x3, waiting for transfers between devices, on_device(): lax.ppermute(raw, 'y', [(i, i ^ k) for i in range(count_y)])  2.95 us
  transfers between devices with their start and end apart: 11, of which 5 were waited for; matrix products, arithmetic and copies ran while one was open for 4% of the time, Pallas kernels for 17%

profile of v5, /device:TPU:6, one launch (start us, length us, event | category | flops | bytes accessed | tf_op | source)
XLA Modules:
  0.0 65.1 jit_solution(6887804564246433290)
XLA Ops:
  0.0 4.5 %shard_map.73.raw = f32[16,256]{1,0:T(8,128)} custom-call(bf16[8,64,192]{2,1,0:T(8,128)(2,1)} %refs_0_.1, bf16[4,3,4,64]{3,2,1,0:T(4,128)(2,1)} %bitcast.16, bf16[4,256,128]{2,1,0:T(8,128)(2,1)} %bitcast.15, bf16[4,512,256]{2,1,0:T(8,128)(2,1)} %bitcast.14, bf16[256,256]{1,0:T(8,128)(2,1)} %refs_4_.1, f32[8,256]{1,0:T(8,128)} %refs_5_.1), custom_call_target="tpu_custom_call" | custom-call | flops 5000000000 | bytes 2000000 | tf_op jit(solution)/shard_map/pallas_call | solution.py:198
  4.5 1.7 %collective-permute-start = (f32[16,256]{1,0:T(8,128)}, f32[16,256]{1,0:T(8,128)S(1)}, u32[]{:S(2)}, u32[]{:S(2)}) collective-permute-start(f32[16,256]{1,0:T(8,128)} %shard_map.73.raw), channel_id=1, source_target_pairs={{0,1},{1,0},{2,3},{3,2},{4,5},{5,4},{6,7},{7,6},{8,9},{9,8},{10,11... | collective-permute-start | bytes 49160 | tf_op jit(solution)/shard_map/ppermute | solution.py:337
  6.2 2.9 %collective-permute-start.1 = (f32[16,256]{1,0:T(8,128)}, f32[16,256]{1,0:T(8,128)S(1)}, u32[]{:S(2)}, u32[]{:S(2)}) collective-permute-start(f32[16,256]{1,0:T(8,128)} %shard_map.73.raw), channel_id=1, source_target_pairs={{0,2},{1,3},{2,0},{3,1},{4,6},{5,7},{6,4},{7,5},{8,10},{9,11},{10,... | collective-permute-start | bytes 49160 | tf_op jit(solution)/shard_map/ppermute | solution.py:337
  9.1 0.2 collective-permute-start.2
  9.3 0.8 %constant_dynamic-update-slice_fusion.3 = (f32[64,256]{1,0:T(8,128)S(1)}, f32[128,256]{1,0:T(8,128)S(1)}) fusion(f32[16,256]{1,0:T(8,128)} %shard_map.73.raw), kind=kLoop, calls=%fused_computation.25 | loop fusion | bytes 49152
  10.1 1.2 %shard_map.74 = (bf16[256,256]{1,0:T(8,128)(2,1)S(1)}, bf16[256,256]{1,0:T(8,128)(2,1)S(1)}) custom-call(f32[256,256]{1,0:T(8,128)S(1)} %copy-done.1), custom_call_target="tpu_custom_call" | custom-call | flops 1000000000 | bytes 1000000 | tf_op jit(solution)/shard_map/pallas_call | solution.py:34
  11.3 0.3 collective-permute-done.1
  11.6 2.6 %collective-permute-done.2 = f32[16,256]{1,0:T(8,128)S(1)} collective-permute-done((f32[16,256]{1,0:T(8,128)}, f32[16,256]{1,0:T(8,128)S(1)}, u32[]{:S(2)}, u32[]{:S(2)}) %collective-permute-start.2) | collective-permute-done | bytes 16416 | tf_op jit(solution)/shard_map/ppermute | solution.py:337
  14.2 1.9 %collective-permute-start.3 = (f32[64,256]{1,0:T(8,128)S(1)}, f32[64,256]{1,0:T(8,128)S(1)}, u32[]{:S(2)}, u32[]{:S(2)}) collective-permute-start(f32[64,256]{1,0:T(8,128)S(1)} %get-tuple-element.57.raw), channel_id=1, source_target_pairs={{0,4},{4,0},{8,12},{12,8},{16,20},{20,16},{24,28},{28,24},{1,5},{5... | collective-permute-start | bytes 196616 | tf_op jit(solution)/shard_map/ppermute | solution.py:339
  16.2 3.8 %shard_map.75 = (f32[264,256]{1,0:T(8,128)S(1)}, f32[264,256]{1,0:T(8,128)S(1)}) custom-call(bf16[256,256]{1,0:T(8,128)(2,1)S(1)} %get-tuple-element.31.top, bf16[256,256]{1,0:T(8,128)(2,1)S(1)} %get-tuple-element.32.rest, f32[64,256]{1,0:T(8,128)S(1)} %get-tuple-element.57.raw), custom_call_target="tpu_custom_call" | custom-call | flops 4000000000 | bytes 2000000 | tf_op jit(solution)/shard_map/pallas_call | solution.py:34
  20.0 3.5 %collective-permute-start.4 = (f32[128,256]{1,0:T(8,128)S(1)}, f32[128,256]{1,0:T(8,128)S(1)}, u32[]{:S(2)}, u32[]{:S(2)}) collective-permute-start(f32[128,256]{1,0:T(8,128)S(1)} %constant_dynamic-update-slice_fusion.4), channel_id=1, source_target_pairs={{0,8},{4,12},{8,0},{12,4},{16,24},{20,28},{24,16},{28,20},{1,9},{5... | collective-permute-start | bytes 393224 | tf_op jit(solution)/shard_map/ppermute | solution.py:342
  23.5 4.2 %shard_map.76 = (f32[264,256]{1,0:T(8,128)S(1)}, f32[264,256]{1,0:T(8,128)S(1)}) custom-call(bf16[256,256]{1,0:T(8,128)(2,1)S(1)} %get-tuple-element.31.top, bf16[256,256]{1,0:T(8,128)(2,1)S(1)} %get-tuple-element.32.rest, f32[64,256]{1,0:T(8,128)S(1)} %collective-permute-done.3.raw, f32[264,256]{1,0:T(8,128)S(1)} %get-tuple-element.36.refs_0_, ...), custom_call_target="tpu_custom_call" | custom-call | flops 4000000000 | bytes 2000000 | tf_op jit(solution)/shard_map/pallas_call | solution.py:34
  27.8 8.2 %shard_map.77 = (f32[264,256]{1,0:T(8,128)S(1)}, f32[264,256]{1,0:T(8,128)S(1)}) custom-call(bf16[256,256]{1,0:T(8,128)(2,1)S(1)} %get-tuple-element.31.top, bf16[256,256]{1,0:T(8,128)(2,1)S(1)} %get-tuple-element.32.rest, f32[128,256]{1,0:T(8,128)S(1)} %collective-permute-done.4.raw, f32[264,256]{1,0:T(8,128)S(1)} %get-tuple-element.40.refs_0_), custom_call_target="tpu_custom_call" | custom-call | flops 8000000000 | bytes 2000000 | tf_op jit(solution)/shard_map/pallas_call | solution.py:34
  35.9 4.2 %collective-permute-start.5 = (f32[264,256]{1,0:T(8,128)S(1)}, f32[264,256]{1,0:T(8,128)S(1)}, u32[]{:S(2)}, u32[]{:S(2)}) collective-permute-start(f32[264,256]{1,0:T(8,128)S(1)} %get-tuple-element.41), channel_id=1, source_target_pairs={{0,24},{4,28},{8,16},{12,20},{16,8},{20,12},{24,0},{28,4},{1,25},{... | collective-permute-start | bytes 811016 | tf_op jit(solution)/shard_map/ppermute | solution.py:348
  40.1 0.3 fusion.own
  40.4 0.4 copy-done
  40.8 2.2 %shard_map.78 = (bf16[256,2048]{1,0:T(8,128)(2,1)S(1)}, bf16[256,2048]{1,0:T(8,128)(2,1)S(1)}, f32[8,256]{1,0:T(8,128)S(1)}) custom-call(bf16[256,256]{1,0:T(8,128)(2,1)S(1)} %get-tuple-element.31.top, bf16[256,256]{1,0:T(8,128)(2,1)S(1)} %get-tuple-element.32.rest, f32[264,256]{1,0:T(8,128)S(1)} %fusion.own, f32[16,256]{1,0:T(8,128)S(1)} %copy-done), custom_call_target="tpu_custom_call" | custom-call | flops 1000000000 | bytes 1000000 | tf_op jit(solution)/shard_map/pallas_call | solution.py:34
  43.1 6.0 %collective-permute-done.5 = f32[264,256]{1,0:T(8,128)S(1)} collective-permute-done((f32[264,256]{1,0:T(8,128)S(1)}, f32[264,256]{1,0:T(8,128)S(1)}, u32[]{:S(2)}, u32[]{:S(2)}) %collective-permute-start.5) | collective-permute-done | bytes 270368 | tf_op jit(solution)/shard_map/ppermute | solution.py:348
  49.1 0.3 convolution_add_fusion.2
  49.4 0.1 collective-permute-start.6
  49.5 1.5 %collective-permute-done.6 = f32[264,256]{1,0:T(8,128)S(1)} collective-permute-done((f32[264,256]{1,0:T(8,128)S(1)}, f32[264,256]{1,0:T(8,128)S(1)}, u32[]{:S(2)}, u32[]{:S(2)}) %collective-permute-start.6) | collective-permute-done | bytes 270368 | tf_op jit(solution)/shard_map/ppermute | solution.py:366
  51.1 0.3 convolution_add_fusion.1
  51.4 1.3 %collective-permute-start.10 = (f32[264,256]{1,0:T(8,128)S(1)}, f32[264,256]{1,0:T(8,128)}, u32[]{:S(2)}, u32[]{:S(2)}) collective-permute-start(f32[264,256]{1,0:T(8,128)S(1)} %convolution_add_fusion.1), channel_id=1, source_target_pairs={{128,192},{129,193},{130,194},{131,195},{132,196},{133,197},{134,1... | collective-permute-start | bytes 811016 | tf_op jit(solution)/shard_map/ppermute | solution.py:370
  52.7 0.7 %collective-permute-start.7 = (f32[1,256]{1,0:T(1,128)S(1)}, f32[1,256]{1,0:T(1,128)S(1)}, u32[]{:S(2)}, u32[]{:S(2)}) collective-permute-start(f32[1,256]{1,0:T(1,128)S(1)} %slice.52), channel_id=1, source_target_pairs={{0,64},{1,65},{2,66},{3,67},{4,68},{5,69},{6,70},{7,71},{8,72},{9,... | collective-permute-start | bytes 3080 | tf_op jit(solution)/shard_map/ppermute | solution.py:372
  53.4 0.3 convolution_add_fusion.late
  53.7 0.1 convolution_add_fusion.5
  53.8 1.3 %collective-permute-start.9 = (f32[1,256]{1,0:T(1,128)S(1)}, f32[1,256]{1,0:T(1,128)S(1)}, u32[]{:S(2)}, u32[]{:S(2)}) collective-permute-start(f32[1,256]{1,0:T(1,128)S(1)} %convolution_add_fusion.5), channel_id=1, source_target_pairs={{64,192},{65,193},{66,194},{67,195},{68,196},{69,197},{70,198},{71... | collective-permute-start | bytes 3080 | tf_op jit(solution)/shard_map/ppermute | solution.py:377
  55.2 0.7 %collective-permute-start.8 = (f32[1,256]{1,0:T(1,128)S(1)}, f32[1,256]{1,0:T(1,128)S(1)}, u32[]{:S(2)}, u32[]{:S(2)}) collective-permute-start(f32[1,256]{1,0:T(1,128)S(1)} %convolution_add_fusion.5), channel_id=1, source_target_pairs={{64,128},{65,129},{66,130},{67,131},{68,132},{69,133},{70,134},{71... | collective-permute-start | bytes 3080 | tf_op jit(solution)/shard_map/ppermute | solution.py:378
  55.9 6.8 %collective-permute-done.9 = f32[1,256]{1,0:T(1,128)S(1)} collective-permute-done((f32[1,256]{1,0:T(1,128)S(1)}, f32[1,256]{1,0:T(1,128)S(1)}, u32[]{:S(2)}, u32[]{:S(2)}) %collective-permute-start.9) | collective-permute-done | bytes 1056 | tf_op jit(solution)/shard_map/ppermute | solution.py:377
  62.7 1.1 %convolution_add_fusion.4 = f32[1,256]{1,0:T(1,128)S(1)} fusion(f32[264,256]{1,0:T(8,128)} %collective-permute-done.10, f32[1,256]{1,0:T(1,128)S(1)} %collective-permute-done.9), kind=kOutput, calls=%fused_computation.5 | convolution fusion | flops 393472 | bytes 265216 | tf_op jit(solution)/shard_map/dot_general | solution.py:312
  63.7 0.0 collective-permute-done.8
  63.8 1.3 %shard_map.79 = f32[8,256]{1,0:T(8,128)} custom-call(f32[1,256]{1,0:T(1,128)S(1)} %broadcast_select_fusion.8.entry, f32[264,256]{1,0:T(8,128)S(1)} %convolution_add_fusion.late, bf16[256,2048]{1,0:T(8,128)(2,1)S(1)} %get-tuple-element.52.maps_top, bf16[256,2048]{1,0:T(8,128)(2,1)S(1)} %get-tuple-element.53.maps_rest, f32[8,256]{1,0:T(8,128)S(1)} %get-tuple-element.54.states), custom_call_target="tpu_custom_call" | custom-call | flops 100000000 | bytes 1000000 | tf_op jit(solution)/shard_map/pallas_call | solution.py:34
  (21 shorter events, 0.2 us)
Async XLA Ops:
  0.0 10.1 %copy-start.1 = (f32[256,256]{1,0:T(8,128)S(1)}, f32[256,256]{1,0:T(8,128)}, u32[]{:S(2)}) copy-start(f32[256,256]{1,0:T(8,128)} %source) | copy-start | bytes 786436
  4.5 6.8 %collective-permute-start = (f32[16,256]{1,0:T(8,128)}, f32[16,256]{1,0:T(8,128)S(1)}, u32[]{:S(2)}, u32[]{:S(2)}) collective-permute-start(f32[16,256]{1,0:T(8,128)} %shard_map.73.raw), channel_id=1, source_target_pairs={{0,1},{1,0},{2,3},{3,2},{4,5},{5,4},{6,7},{7,6},{8,9},{9,8},{10,11... | collective-permute-start | bytes 49160 | tf_op jit(solution)/shard_map/ppermute | solution.py:337
  6.2 5.5 %collective-permute-start.1 = (f32[16,256]{1,0:T(8,128)}, f32[16,256]{1,0:T(8,128)S(1)}, u32[]{:S(2)}, u32[]{:S(2)}) collective-permute-start(f32[16,256]{1,0:T(8,128)} %shard_map.73.raw), channel_id=1, source_target_pairs={{0,2},{1,3},{2,0},{3,1},{4,6},{5,7},{6,4},{7,5},{8,10},{9,11},{10,... | collective-permute-start | bytes 49160 | tf_op jit(solution)/shard_map/ppermute | solution.py:337
  9.1 5.2 %collective-permute-start.2 = (f32[16,256]{1,0:T(8,128)}, f32[16,256]{1,0:T(8,128)S(1)}, u32[]{:S(2)}, u32[]{:S(2)}) collective-permute-start(f32[16,256]{1,0:T(8,128)} %shard_map.73.raw), channel_id=1, source_target_pairs={{0,3},{1,2},{2,1},{3,0},{4,7},{5,6},{6,5},{7,4},{8,11},{9,10},{10,... | collective-permute-start | bytes 49160 | tf_op jit(solution)/shard_map/ppermute | solution.py:337
  14.2 5.7 %collective-permute-start.3 = (f32[64,256]{1,0:T(8,128)S(1)}, f32[64,256]{1,0:T(8,128)S(1)}, u32[]{:S(2)}, u32[]{:S(2)}) collective-permute-start(f32[64,256]{1,0:T(8,128)S(1)} %get-tuple-element.57.raw), channel_id=1, source_target_pairs={{0,4},{4,0},{8,12},{12,8},{16,20},{20,16},{24,28},{28,24},{1,5},{5... | collective-permute-start | bytes 196616 | tf_op jit(solution)/shard_map/ppermute | solution.py:339
  20.0 7.7 %collective-permute-start.4 = (f32[128,256]{1,0:T(8,128)S(1)}, f32[128,256]{1,0:T(8,128)S(1)}, u32[]{:S(2)}, u32[]{:S(2)}) collective-permute-start(f32[128,256]{1,0:T(8,128)S(1)} %constant_dynamic-update-slice_fusion.4), channel_id=1, source_target_pairs={{0,8},{4,12},{8,0},{12,4},{16,24},{20,28},{24,16},{28,20},{1,9},{5... | collective-permute-start | bytes 393224 | tf_op jit(solution)/shard_map/ppermute | solution.py:342
  35.9 13.2 %collective-permute-start.5 = (f32[264,256]{1,0:T(8,128)S(1)}, f32[264,256]{1,0:T(8,128)S(1)}, u32[]{:S(2)}, u32[]{:S(2)}) collective-permute-start(f32[264,256]{1,0:T(8,128)S(1)} %get-tuple-element.41), channel_id=1, source_target_pairs={{0,24},{4,28},{8,16},{12,20},{16,8},{20,12},{24,0},{28,4},{1,25},{... | collective-permute-start | bytes 811016 | tf_op jit(solution)/shard_map/ppermute | solution.py:348
  40.1 0.7 %copy-start = (f32[16,256]{1,0:T(8,128)S(1)}, f32[16,256]{1,0:T(8,128)}, u32[]{:S(2)}) copy-start(f32[16,256]{1,0:T(8,128)} %shard_map.73.raw) | copy-start | bytes 49156
  49.4 1.6 %collective-permute-start.6 = (f32[264,256]{1,0:T(8,128)S(1)}, f32[264,256]{1,0:T(8,128)S(1)}, u32[]{:S(2)}, u32[]{:S(2)}) collective-permute-start(f32[264,256]{1,0:T(8,128)S(1)} %convolution_add_fusion.2), channel_id=1, source_target_pairs={{0,32},{32,0},{1,33},{33,1},{2,34},{34,2},{3,35},{35,3},{4,36},{36... | collective-permute-start | bytes 811016 | tf_op jit(solution)/shard_map/ppermute | solution.py:366
  51.4 11.2 %collective-permute-start.10 = (f32[264,256]{1,0:T(8,128)S(1)}, f32[264,256]{1,0:T(8,128)}, u32[]{:S(2)}, u32[]{:S(2)}) collective-permute-start(f32[264,256]{1,0:T(8,128)S(1)} %convolution_add_fusion.1), channel_id=1, source_target_pairs={{128,192},{129,193},{130,194},{131,195},{132,196},{133,197},{134,1... | collective-permute-start | bytes 811016 | tf_op jit(solution)/shard_map/ppermute | solution.py:370
  52.7 1.0 %collective-permute-start.7 = (f32[1,256]{1,0:T(1,128)S(1)}, f32[1,256]{1,0:T(1,128)S(1)}, u32[]{:S(2)}, u32[]{:S(2)}) collective-permute-start(f32[1,256]{1,0:T(1,128)S(1)} %slice.52), channel_id=1, source_target_pairs={{0,64},{1,65},{2,66},{3,67},{4,68},{5,69},{6,70},{7,71},{8,72},{9,... | collective-permute-start | bytes 3080 | tf_op jit(solution)/shard_map/ppermute | solution.py:372
  53.8 8.8 %collective-permute-start.9 = (f32[1,256]{1,0:T(1,128)S(1)}, f32[1,256]{1,0:T(1,128)S(1)}, u32[]{:S(2)}, u32[]{:S(2)}) collective-permute-start(f32[1,256]{1,0:T(1,128)S(1)} %convolution_add_fusion.5), channel_id=1, source_target_pairs={{64,192},{65,193},{66,194},{67,195},{68,196},{69,197},{70,198},{71... | collective-permute-start | bytes 3080 | tf_op jit(solution)/shard_map/ppermute | solution.py:377
  55.2 8.6 %collective-permute-start.8 = (f32[1,256]{1,0:T(1,128)S(1)}, f32[1,256]{1,0:T(1,128)S(1)}, u32[]{:S(2)}, u32[]{:S(2)}) collective-permute-start(f32[1,256]{1,0:T(1,128)S(1)} %convolution_add_fusion.5), channel_id=1, source_target_pairs={{64,128},{65,129},{66,130},{67,131},{68,132},{69,133},{70,134},{71... | collective-permute-start | bytes 3080 | tf_op jit(solution)/shard_map/ppermute | solution.py:378

commit v6 on v4

--- a/solution.py
+++ b/solution.py
@@ -368,7 +368,7 @@
     block_end = dot(low_core[width : width + 1], high_core[:width]) + high_core[width : width + 1]
     block_end, low_core = lax.optimization_barrier((block_end, low_core))
 
-    first_end = lax.ppermute(block_end, "x", [(0, 1)])
+    first_end = lax.ppermute(block_end, "x", [(i, i ^ 1) for i in range(count_x)])
     block = join(low_core, high_core)
     third = lax.ppermute(block, "x", [(2, 3)])
     still = jnp.concatenate([jnp.eye(width, dtype=F32), jnp.zeros((8, width), F32)], 0)

time: 64.9 us -> 64.8 us (level)
    ppermute x1, waiting for transfers between devices: 1.5 us -> 0.53 us  [on_device(): third = lax.ppermute(block, 'x', [(2, 3)])]
    ppermute x1, waiting for transfers between devices: 0.01 us -> 0.86 us  [on_device(): lax.ppermute(block_end, 'x', [(i, i ^ 1) for i in range(count_x)])]
  transfers between devices with their start and end apart: 11 -> 11, of which waited for: 6 -> 7; matrix products, arithmetic and copies ran while one was open for 2% -> 2% of each run, Pallas kernels for 18% -> 18%
where the time goes in v6:
time: 64.8 us; the launch traced here: 64.1 us
  Pallas kernels  25.3 us (39%)
  starting transfers between devices  18.7 us (29%)
  waiting for transfers between devices  18 us (28%)
  matrix products  1.55 us (2%)
    pallas_call x6, Pallas kernels, call(): pl.pallas_call(kernel, out_shape=[jax.ShapeDtypeStruct(shape, kind) for s...  20.8 us
    ppermute x1, waiting for transfers between devices, on_device(): other = lax.ppermute(block, 'z', [(i, i ^ 6) for i in range(count_z)])  6.44 us
    ppermute x1, waiting for transfers between devices, on_device(): for_fourth = lax.ppermute(leaving, 'x', [(1, 3)])  4.99 us
    ppermute x3, starting transfers between devices, on_device(): lax.ppermute(raw, 'y', [(i, i ^ k) for i in range(count_y)])  4.79 us
    pallas_call x1, Pallas kernels, encode(): pl.pallas_call(encoder_kernel, out_shape=jax.ShapeDtypeStruct((2 * local,...  4.51 us
    ppermute x1, starting transfers between devices, on_device(): other = lax.ppermute(block, 'z', [(i, i ^ 6) for i in range(count_z)])  4.19 us
    ppermute x3, waiting for transfers between devices, on_device(): lax.ppermute(raw, 'y', [(i, i ^ k) for i in range(count_y)])  3.68 us
    ppermute x1, starting transfers between devices, on_device(): lax.ppermute(jnp.concatenate([rows, beside], 0), 'z', exchange_pairs(2, c...  3.54 us
  transfers between devices with their start and end apart: 11, of which 7 were waited for; matrix products, arithmetic and copies ran while one was open for 2% of the time, Pallas kernels for 18%

profile of v6, /device:TPU:6, one launch (start us, length us, event | category | flops | bytes accessed | tf_op | source)
XLA Modules:
  0.0 64.1 jit_solution(10337895834992838232)
XLA Ops:
  0.0 4.5 %shard_map.73.raw = f32[16,256]{1,0:T(8,128)} custom-call(bf16[8,64,192]{2,1,0:T(8,128)(2,1)} %refs_0_.1, bf16[4,3,4,64]{3,2,1,0:T(4,128)(2,1)} %bitcast.22, bf16[4,256,128]{2,1,0:T(8,128)(2,1)} %bitcast.21, bf16[4,512,256]{2,1,0:T(8,128)(2,1)} %bitcast.20, bf16[256,256]{1,0:T(8,128)(2,1)} %refs_4_.1, f32[8,256]{1,0:T(8,128)} %refs_5_.1), custom_call_target="tpu_custom_call" | custom-call | flops 5000000000 | bytes 2000000 | tf_op jit(solution)/shard_map/pallas_call | solution.py:198
  4.5 1.7 %collective-permute-start = (f32[16,256]{1,0:T(8,128)}, f32[16,256]{1,0:T(8,128)S(1)}, u32[]{:S(2)}, u32[]{:S(2)}) collective-permute-start(f32[16,256]{1,0:T(8,128)} %shard_map.73.raw), channel_id=1, source_target_pairs={{0,1},{1,0},{2,3},{3,2},{4,5},{5,4},{6,7},{7,6},{8,9},{9,8},{10,11... | collective-permute-start | bytes 49160 | tf_op jit(solution)/shard_map/ppermute | solution.py:337
  6.2 2.9 %collective-permute-start.1 = (f32[16,256]{1,0:T(8,128)}, f32[16,256]{1,0:T(8,128)S(1)}, u32[]{:S(2)}, u32[]{:S(2)}) collective-permute-start(f32[16,256]{1,0:T(8,128)} %shard_map.73.raw), channel_id=1, source_target_pairs={{0,2},{1,3},{2,0},{3,1},{4,6},{5,7},{6,4},{7,5},{8,10},{9,11},{10,... | collective-permute-start | bytes 49160 | tf_op jit(solution)/shard_map/ppermute | solution.py:337
  9.1 0.2 collective-permute-start.2
  9.4 1.2 %shard_map.74 = (bf16[256,256]{1,0:T(8,128)(2,1)S(1)}, bf16[256,256]{1,0:T(8,128)(2,1)S(1)}) custom-call(f32[256,256]{1,0:T(8,128)S(1)} %copy-done.1), custom_call_target="tpu_custom_call" | custom-call | flops 1000000000 | bytes 1000000 | tf_op jit(solution)/shard_map/pallas_call | solution.py:34
  10.6 1.1 %collective-permute-done.1 = f32[16,256]{1,0:T(8,128)S(1)} collective-permute-done((f32[16,256]{1,0:T(8,128)}, f32[16,256]{1,0:T(8,128)S(1)}, u32[]{:S(2)}, u32[]{:S(2)}) %collective-permute-start.1) | collective-permute-done | bytes 16416 | tf_op jit(solution)/shard_map/ppermute | solution.py:337
  11.7 2.6 %collective-permute-done.2 = f32[16,256]{1,0:T(8,128)S(1)} collective-permute-done((f32[16,256]{1,0:T(8,128)}, f32[16,256]{1,0:T(8,128)S(1)}, u32[]{:S(2)}, u32[]{:S(2)}) %collective-permute-start.2) | collective-permute-done | bytes 16416 | tf_op jit(solution)/shard_map/ppermute | solution.py:337
  14.3 1.9 %collective-permute-start.3 = (f32[64,256]{1,0:T(8,128)S(1)}, f32[64,256]{1,0:T(8,128)S(1)}, u32[]{:S(2)}, u32[]{:S(2)}) collective-permute-start(f32[64,256]{1,0:T(8,128)S(1)} %get-tuple-element.63.raw), channel_id=1, source_target_pairs={{0,4},{4,0},{8,12},{12,8},{16,20},{20,16},{24,28},{28,24},{1,5},{5... | collective-permute-start | bytes 196616 | tf_op jit(solution)/shard_map/ppermute | solution.py:339
  16.2 3.8 %shard_map.75 = (f32[264,256]{1,0:T(8,128)S(1)}, f32[264,256]{1,0:T(8,128)S(1)}) custom-call(bf16[256,256]{1,0:T(8,128)(2,1)S(1)} %get-tuple-element.33.top, bf16[256,256]{1,0:T(8,128)(2,1)S(1)} %get-tuple-element.34.rest, f32[64,256]{1,0:T(8,128)S(1)} %get-tuple-element.63.raw), custom_call_target="tpu_custom_call" | custom-call | flops 4000000000 | bytes 2000000 | tf_op jit(solution)/shard_map/pallas_call | solution.py:34
  20.0 3.5 %collective-permute-start.4 = (f32[128,256]{1,0:T(8,128)S(1)}, f32[128,256]{1,0:T(8,128)S(1)}, u32[]{:S(2)}, u32[]{:S(2)}) collective-permute-start(f32[128,256]{1,0:T(8,128)S(1)} %constant_dynamic-update-slice_fusion.4), channel_id=1, source_target_pairs={{0,8},{4,12},{8,0},{12,4},{16,24},{20,28},{24,16},{28,20},{1,9},{5... | collective-permute-start | bytes 393224 | tf_op jit(solution)/shard_map/ppermute | solution.py:342
  23.6 4.2 %shard_map.76 = (f32[264,256]{1,0:T(8,128)S(1)}, f32[264,256]{1,0:T(8,128)S(1)}) custom-call(bf16[256,256]{1,0:T(8,128)(2,1)S(1)} %get-tuple-element.33.top, bf16[256,256]{1,0:T(8,128)(2,1)S(1)} %get-tuple-element.34.rest, f32[64,256]{1,0:T(8,128)S(1)} %collective-permute-done.3.raw, f32[264,256]{1,0:T(8,128)S(1)} %get-tuple-element.38.refs_0_, ...), custom_call_target="tpu_custom_call" | custom-call | flops 4000000000 | bytes 2000000 | tf_op jit(solution)/shard_map/pallas_call | solution.py:34
  27.8 8.2 %shard_map.77 = (f32[264,256]{1,0:T(8,128)S(1)}, f32[264,256]{1,0:T(8,128)S(1)}) custom-call(bf16[256,256]{1,0:T(8,128)(2,1)S(1)} %get-tuple-element.33.top, bf16[256,256]{1,0:T(8,128)(2,1)S(1)} %get-tuple-element.34.rest, f32[128,256]{1,0:T(8,128)S(1)} %collective-permute-done.4.raw, f32[264,256]{1,0:T(8,128)S(1)} %get-tuple-element.42.refs_0_), custom_call_target="tpu_custom_call" | custom-call | flops 8000000000 | bytes 2000000 | tf_op jit(solution)/shard_map/pallas_call | solution.py:34
  36.0 4.2 %collective-permute-start.5 = (f32[264,256]{1,0:T(8,128)S(1)}, f32[264,256]{1,0:T(8,128)S(1)}, u32[]{:S(2)}, u32[]{:S(2)}) collective-permute-start(f32[264,256]{1,0:T(8,128)S(1)} %get-tuple-element.43), channel_id=1, source_target_pairs={{0,24},{4,28},{8,16},{12,20},{16,8},{20,12},{24,0},{28,4},{1,25},{... | collective-permute-start | bytes 811016 | tf_op jit(solution)/shard_map/ppermute | solution.py:348
  40.1 0.3 fusion.own
  40.4 2.2 %shard_map.78 = (bf16[256,2048]{1,0:T(8,128)(2,1)S(1)}, bf16[256,2048]{1,0:T(8,128)(2,1)S(1)}, f32[8,256]{1,0:T(8,128)S(1)}) custom-call(bf16[256,256]{1,0:T(8,128)(2,1)S(1)} %get-tuple-element.33.top, bf16[256,256]{1,0:T(8,128)(2,1)S(1)} %get-tuple-element.34.rest, f32[264,256]{1,0:T(8,128)S(1)} %fusion.own, f32[16,256]{1,0:T(8,128)S(1)} %copy-done), custom_call_target="tpu_custom_call" | custom-call | flops 1000000000 | bytes 1000000 | tf_op jit(solution)/shard_map/pallas_call | solution.py:34
  42.7 6.4 %collective-permute-done.5 = f32[264,256]{1,0:T(8,128)S(1)} collective-permute-done((f32[264,256]{1,0:T(8,128)S(1)}, f32[264,256]{1,0:T(8,128)S(1)}, u32[]{:S(2)}, u32[]{:S(2)}) %collective-permute-start.5) | collective-permute-done | bytes 270368 | tf_op jit(solution)/shard_map/ppermute | solution.py:348
  49.2 0.3 convolution_add_fusion.2
  49.4 0.1 collective-permute-start.6
  49.6 1.5 %collective-permute-done.6 = f32[264,256]{1,0:T(8,128)S(1)} collective-permute-done((f32[264,256]{1,0:T(8,128)S(1)}, f32[264,256]{1,0:T(8,128)S(1)}, u32[]{:S(2)}, u32[]{:S(2)}) %collective-permute-start.6) | collective-permute-done | bytes 270368 | tf_op jit(solution)/shard_map/ppermute | solution.py:366
  51.1 0.1 convolution_add_fusion.6
  51.3 0.9 %collective-permute-start.7 = (f32[1,256]{1,0:T(1,128)S(1)}, f32[1,256]{1,0:T(1,128)S(1)}, u32[]{:S(2)}, u32[]{:S(2)}) collective-permute-start(f32[1,256]{1,0:T(1,128)S(1)} %convolution_add_fusion.6), channel_id=1, source_target_pairs={{0,64},{64,0},{128,192},{192,128},{1,65},{65,1},{129,193},{193,129... | collective-permute-start | bytes 3080 | tf_op jit(solution)/shard_map/ppermute | solution.py:371
  52.2 0.3 convolution_add_fusion
  52.4 1.3 %collective-permute-start.10 = (f32[264,256]{1,0:T(8,128)S(1)}, f32[264,256]{1,0:T(8,128)S(1)}, u32[]{:S(2)}, u32[]{:S(2)}) collective-permute-start(f32[264,256]{1,0:T(8,128)S(1)} %convolution_add_fusion), channel_id=1, source_target_pairs={{128,192},{129,193},{130,194},{131,195},{132,196},{133,197},{134,1... | collective-permute-start | bytes 811016 | tf_op jit(solution)/shard_map/ppermute | solution.py:373
  53.7 0.3 convolution_add_fusion.1.late
  54.0 0.9 %collective-permute-done.7 = f32[1,256]{1,0:T(1,128)S(1)} collective-permute-done((f32[1,256]{1,0:T(1,128)S(1)}, f32[1,256]{1,0:T(1,128)S(1)}, u32[]{:S(2)}, u32[]{:S(2)}) %collective-permute-start.7) | collective-permute-done | bytes 1056 | tf_op jit(solution)/shard_map/ppermute | solution.py:371
  54.9 0.1 convolution_add_fusion.5
  55.0 1.3 %collective-permute-start.9 = (f32[1,256]{1,0:T(1,128)S(1)}, f32[1,256]{1,0:T(1,128)S(1)}, u32[]{:S(2)}, u32[]{:S(2)}) collective-permute-start(f32[1,256]{1,0:T(1,128)S(1)} %convolution_add_fusion.5), channel_id=1, source_target_pairs={{64,192},{65,193},{66,194},{67,195},{68,196},{69,197},{70,198},{71... | collective-permute-start | bytes 3080 | tf_op jit(solution)/shard_map/ppermute | solution.py:378
  56.4 0.7 %collective-permute-start.8 = (f32[1,256]{1,0:T(1,128)S(1)}, f32[1,256]{1,0:T(1,128)S(1)}, u32[]{:S(2)}, u32[]{:S(2)}) collective-permute-start(f32[1,256]{1,0:T(1,128)S(1)} %convolution_add_fusion.5), channel_id=1, source_target_pairs={{64,128},{65,129},{66,130},{67,131},{68,132},{69,133},{70,134},{71... | collective-permute-start | bytes 3080 | tf_op jit(solution)/shard_map/ppermute | solution.py:379
  57.1 5.0 %collective-permute-done.9 = f32[1,256]{1,0:T(1,128)S(1)} collective-permute-done((f32[1,256]{1,0:T(1,128)S(1)}, f32[1,256]{1,0:T(1,128)S(1)}, u32[]{:S(2)}, u32[]{:S(2)}) %collective-permute-start.9) | collective-permute-done | bytes 1056 | tf_op jit(solution)/shard_map/ppermute | solution.py:378
  62.0 0.5 collective-permute-done.10
  62.6 0.1 convolution_add_fusion.4
  62.8 1.3 %shard_map.79 = f32[8,256]{1,0:T(8,128)} custom-call(f32[1,256]{1,0:T(1,128)S(1)} %broadcast_select_fusion.6.entry, f32[264,256]{1,0:T(8,128)S(1)} %convolution_add_fusion.1.late, bf16[256,2048]{1,0:T(8,128)(2,1)S(1)} %get-tuple-element.56.maps_top, bf16[256,2048]{1,0:T(8,128)(2,1)S(1)} %get-tuple-element.57.maps_rest, f32[8,256]{1,0:T(8,128)S(1)} %get-tuple-element.58.states), custom_call_target="tpu_custom_call" | custom-call | flops 100000000 | bytes 1000000 | tf_op jit(solution)/shard_map/pallas_call | solution.py:34
  (21 shorter events, 0.2 us)
Async XLA Ops:
  0.0 9.4 %copy-start.1 = (f32[256,256]{1,0:T(8,128)S(1)}, f32[256,256]{1,0:T(8,128)}, u32[]{:S(2)}) copy-start(f32[256,256]{1,0:T(8,128)} %source) | copy-start | bytes 786436
  4.5 4.8 %copy-start = (f32[16,256]{1,0:T(8,128)S(1)}, f32[16,256]{1,0:T(8,128)}, u32[]{:S(2)}) copy-start(f32[16,256]{1,0:T(8,128)} %shard_map.73.raw) | copy-start | bytes 49156
  4.5 6.0 %collective-permute-start = (f32[16,256]{1,0:T(8,128)}, f32[16,256]{1,0:T(8,128)S(1)}, u32[]{:S(2)}, u32[]{:S(2)}) collective-permute-start(f32[16,256]{1,0:T(8,128)} %shard_map.73.raw), channel_id=1, source_target_pairs={{0,1},{1,0},{2,3},{3,2},{4,5},{5,4},{6,7},{7,6},{8,9},{9,8},{10,11... | collective-permute-start | bytes 49160 | tf_op jit(solution)/shard_map/ppermute | solution.py:337
  6.2 5.5 %collective-permute-start.1 = (f32[16,256]{1,0:T(8,128)}, f32[16,256]{1,0:T(8,128)S(1)}, u32[]{:S(2)}, u32[]{:S(2)}) collective-permute-start(f32[16,256]{1,0:T(8,128)} %shard_map.73.raw), channel_id=1, source_target_pairs={{0,2},{1,3},{2,0},{3,1},{4,6},{5,7},{6,4},{7,5},{8,10},{9,11},{10,... | collective-permute-start | bytes 49160 | tf_op jit(solution)/shard_map/ppermute | solution.py:337
  9.1 5.2 %collective-permute-start.2 = (f32[16,256]{1,0:T(8,128)}, f32[16,256]{1,0:T(8,128)S(1)}, u32[]{:S(2)}, u32[]{:S(2)}) collective-permute-start(f32[16,256]{1,0:T(8,128)} %shard_map.73.raw), channel_id=1, source_target_pairs={{0,3},{1,2},{2,1},{3,0},{4,7},{5,6},{6,5},{7,4},{8,11},{9,10},{10,... | collective-permute-start | bytes 49160 | tf_op jit(solution)/shard_map/ppermute | solution.py:337
  14.3 5.7 %collective-permute-start.3 = (f32[64,256]{1,0:T(8,128)S(1)}, f32[64,256]{1,0:T(8,128)S(1)}, u32[]{:S(2)}, u32[]{:S(2)}) collective-permute-start(f32[64,256]{1,0:T(8,128)S(1)} %get-tuple-element.63.raw), channel_id=1, source_target_pairs={{0,4},{4,0},{8,12},{12,8},{16,20},{20,16},{24,28},{28,24},{1,5},{5... | collective-permute-start | bytes 196616 | tf_op jit(solution)/shard_map/ppermute | solution.py:339
  20.0 7.7 %collective-permute-start.4 = (f32[128,256]{1,0:T(8,128)S(1)}, f32[128,256]{1,0:T(8,128)S(1)}, u32[]{:S(2)}, u32[]{:S(2)}) collective-permute-start(f32[128,256]{1,0:T(8,128)S(1)} %constant_dynamic-update-slice_fusion.4), channel_id=1, source_target_pairs={{0,8},{4,12},{8,0},{12,4},{16,24},{20,28},{24,16},{28,20},{1,9},{5... | collective-permute-start | bytes 393224 | tf_op jit(solution)/shard_map/ppermute | solution.py:342
  36.0 13.2 %collective-permute-start.5 = (f32[264,256]{1,0:T(8,128)S(1)}, f32[264,256]{1,0:T(8,128)S(1)}, u32[]{:S(2)}, u32[]{:S(2)}) collective-permute-start(f32[264,256]{1,0:T(8,128)S(1)} %get-tuple-element.43), channel_id=1, source_target_pairs={{0,24},{4,28},{8,16},{12,20},{16,8},{20,12},{24,0},{28,4},{1,25},{... | collective-permute-start | bytes 811016 | tf_op jit(solution)/shard_map/ppermute | solution.py:348
  49.4 1.6 %collective-permute-start.6 = (f32[264,256]{1,0:T(8,128)S(1)}, f32[264,256]{1,0:T(8,128)S(1)}, u32[]{:S(2)}, u32[]{:S(2)}) collective-permute-start(f32[264,256]{1,0:T(8,128)S(1)} %convolution_add_fusion.2), channel_id=1, source_target_pairs={{0,32},{32,0},{1,33},{33,1},{2,34},{34,2},{3,35},{35,3},{4,36},{36... | collective-permute-start | bytes 811016 | tf_op jit(solution)/shard_map/ppermute | solution.py:366
  51.3 3.6 %collective-permute-start.7 = (f32[1,256]{1,0:T(1,128)S(1)}, f32[1,256]{1,0:T(1,128)S(1)}, u32[]{:S(2)}, u32[]{:S(2)}) collective-permute-start(f32[1,256]{1,0:T(1,128)S(1)} %convolution_add_fusion.6), channel_id=1, source_target_pairs={{0,64},{64,0},{128,192},{192,128},{1,65},{65,1},{129,193},{193,129... | collective-permute-start | bytes 3080 | tf_op jit(solution)/shard_map/ppermute | solution.py:371
  52.4 10.1 %collective-permute-start.10 = (f32[264,256]{1,0:T(8,128)S(1)}, f32[264,256]{1,0:T(8,128)S(1)}, u32[]{:S(2)}, u32[]{:S(2)}) collective-permute-start(f32[264,256]{1,0:T(8,128)S(1)} %convolution_add_fusion), channel_id=1, source_target_pairs={{128,192},{129,193},{130,194},{131,195},{132,196},{133,197},{134,1... | collective-permute-start | bytes 811016 | tf_op jit(solution)/shard_map/ppermute | solution.py:373
  55.0 7.0 %collective-permute-start.9 = (f32[1,256]{1,0:T(1,128)S(1)}, f32[1,256]{1,0:T(1,128)S(1)}, u32[]{:S(2)}, u32[]{:S(2)}) collective-permute-start(f32[1,256]{1,0:T(1,128)S(1)} %convolution_add_fusion.5), channel_id=1, source_target_pairs={{64,192},{65,193},{66,194},{67,195},{68,196},{69,197},{70,198},{71... | collective-permute-start | bytes 3080 | tf_op jit(solution)/shard_map/ppermute | solution.py:378
  56.4 6.3 %collective-permute-start.8 = (f32[1,256]{1,0:T(1,128)S(1)}, f32[1,256]{1,0:T(1,128)S(1)}, u32[]{:S(2)}, u32[]{:S(2)}) collective-permute-start(f32[1,256]{1,0:T(1,128)S(1)} %convolution_add_fusion.5), channel_id=1, source_target_pairs={{64,128},{65,129},{66,130},{67,131},{68,132},{69,133},{70,134},{71... | collective-permute-start | bytes 3080 | tf_op jit(solution)/shard_map/ppermute | solution.py:379
